TPU v7x, 32 devices: a whole 2x2x4 slice. The times are simulated.
32 devices in a mesh: lon: 16 (over z, x, core), lat: 2 (over y).
Axes of the slice: x: 2, y: 2, z: 4, core: 2. Of those that a mesh axis runs over, the one named last changes fastest.
Arguments:
- inputs: bfloat16 [96, 768, 128], P('lat', 'lon'), may hold values from -6 to 6
- weight: bfloat16 [3, 3, 128, 128], replicated, may hold values from -0.1875 to 0.1875
- bias: float32 [128], replicated, may hold values from -3 to 3
- cotangent: bfloat16 [96, 768, 128], P('lat', 'lon'), may hold values from -6 to 6
Outputs:
- outputs: bfloat16 [96, 768, 128], P('lat', 'lon')
- input_grad: bfloat16 [96, 768, 128], P('lat', 'lon')
- weight_grad: float32 [3, 3, 128, 128], replicated
- bias_grad: float32 [128], replicated
All inputs are finite; a program needn't handle non-finite values.
Results may differ from a plain program's by a relative error of at most 0.006.
Values may be sent and summed in bfloat16 or wider, within the bound.
A program may use at most 64 MiB of HBM per device.

v0:
```python
import jax
import jax.numpy as jnp
from jax import lax
from jax.sharding import PartitionSpec as P


def extended(cells, sides, width, closed):
    for axis, dim in sides:
        count = lax.axis_size(axis)
        ends = count if closed else count - 1
        head = lax.slice_in_dim(cells, 0, width, axis=dim)
        tail = lax.slice_in_dim(cells, cells.shape[dim] - width, cells.shape[dim], axis=dim)
        cells = jnp.concatenate(
            [
                lax.ppermute(tail, axis, [(i, (i + 1) % count) for i in range(ends)]),
                cells,
                lax.ppermute(head, axis, [((i + 1) % count, i) for i in range(ends)]),
            ],
            axis=dim,
        )
    return cells


def from_behind(value, axis, steps):
    count = lax.axis_size(axis)
    pairs = [(source, (source + steps) % count) for source in range(count)]
    return lax.ppermute(value, axis, pairs)


def shards(inputs, weight, bias, cotangent):
    rows, cols, chans = inputs.shape
    band = lax.axis_index("lat")
    bands = lax.axis_size("lat")
    half = lax.axis_size("lon") // 2
    wide = extended(inputs, (("lon", 1),), 1, True)
    tall = extended(wide, (("lat", 0),), 1, False)
    far_top, far_bottom = from_behind((wide[0], wide[-1]), "lon", half)
    top = jnp.where(band == 0, far_top, tall[0])
    bottom = jnp.where(band == bands - 1, far_bottom, tall[-1])
    padded = jnp.concatenate([top[None], tall[1:-1], bottom[None]], axis=0)
    pre = jnp.zeros((rows * cols, chans), jnp.float32) + bias[None, :]
    for tap_a in range(3):
        for tap_b in range(3):
            window = padded[tap_a : tap_a + rows, tap_b : tap_b + cols].reshape(rows * cols, chans)
            pre = pre + jnp.dot(window, weight[tap_a, tap_b], preferred_element_type=jnp.float32)
    sig = jax.nn.sigmoid(pre)
    outputs = (pre * sig).astype(jnp.bfloat16).reshape(rows, cols, chans)
    flat_cot = cotangent.reshape(rows * cols, chans).astype(jnp.float32)
    pre_grad = (flat_cot * sig * (1.0 + pre * (1.0 - sig))).astype(jnp.bfloat16)
    padded_grad = jnp.zeros((rows + 2, cols + 2, chans), jnp.float32)
    taps = []
    for tap_a in range(3):
        for tap_b in range(3):
            back = jnp.dot(pre_grad, weight[tap_a, tap_b].T, preferred_element_type=jnp.float32)
            padded_grad = padded_grad.at[tap_a : tap_a + rows, tap_b : tap_b + cols].add(
                back.reshape(rows, cols, chans)
            )
            window = padded[tap_a : tap_a + rows, tap_b : tap_b + cols].reshape(rows * cols, chans)
            taps.append(
                lax.dot_general(
                    window, pre_grad, (((0,), (0,)), ((), ())), preferred_element_type=jnp.float32
                )
            )
    kernel_terms = jnp.concatenate(taps, axis=0)
    bias_terms = jnp.sum(pre_grad.astype(jnp.float32), axis=0)[None, :]
    edges = jnp.stack([padded_grad[0], padded_grad[-1]], axis=0)
    beside_all = extended(edges.astype(jnp.bfloat16), (("lat", 0),), 1, False).astype(edges.dtype)
    polar_top, polar_bottom = (
        from_behind(padded_grad[0].astype(jnp.bfloat16), "lon", half).astype(jnp.float32),
        from_behind(padded_grad[-1].astype(jnp.bfloat16), "lon", half).astype(jnp.float32),
    )
    inner = padded_grad[1:-1]
    inner = inner.at[0].add(beside_all[0] + jnp.where(band == 0, polar_top, 0.0))
    inner = inner.at[-1].add(beside_all[3] + jnp.where(band == bands - 1, polar_bottom, 0.0))
    sides = jnp.stack([inner[:, 0], inner[:, -1]], axis=1)
    beside = extended(sides.astype(jnp.bfloat16), (("lon", 1),), 1, True).astype(sides.dtype)
    core = inner[:, 1:-1]
    core = core.at[:, 0].add(beside[:, 0])
    core = core.at[:, -1].add(beside[:, 3])
    input_grad = core.astype(jnp.bfloat16)
    kernel_sum, bias_sum = lax.psum((kernel_terms, bias_terms), ("lon", "lat"))
    total_cells = rows * cols * lax.axis_size("lon") * lax.axis_size("lat")
    scale = 1.0 / jnp.sqrt(jnp.float32(total_cells))
    weight_grad = kernel_sum.reshape(3, 3, chans, chans) * scale
    bias_grad = bias_sum[0] * scale
    return (outputs, input_grad, weight_grad, bias_grad)


def solution(mesh):
    in_specs = (P("lat", "lon", None), P(), P(), P("lat", "lon", None))
    out_specs = (P("lat", "lon", None), P("lat", "lon", None), P(), P())
    return jax.shard_map(shards, mesh=mesh, in_specs=in_specs, out_specs=out_specs, check_vma=False)
```

profile of v0, /device:TPU:0, one launch (start us, length us, event | category | flops | bytes accessed | tf_op | source)
XLA Modules:
  0.0 252.8 jit_solution(4919324580886464768)
XLA Ops:
  7.2 1.0 fusion.60
  8.8 5.0 %collective-permute-start.1 = (bf16[48,1,128]{2,1,0:T(2,128)(2,1)S(1)}, bf16[48,1,128]{2,1,0:T(2,128)(2,1)S(1)}, u32[]{:S(2)}, u32[]{:S(2)}) collective-permute-start(bf16[48,1,128]{2,1,0:T(2,128)(2,1)S(1)} %get-tuple-element.180), channel_id=1, source_target_pairs={{2,0},{4,2},{6,4},{8,6},{10,8},{12,10},{14,12},{16,14},{18,16},{20... | collective-permute-start | bytes 36872 | tf_op jit(solution)/shard_map/ppermute | solution.py:17
  14.5 1.4 fusion.22
  17.2 3.8 %collective-permute-start.3 = (bf16[1,50,128]{2,1,0:T(8,128)(2,1)S(1)}, bf16[1,50,128]{2,1,0:T(8,128)(2,1)S(1)}, u32[]{:S(2)}, u32[]{:S(2)}) collective-permute-start(bf16[1,50,128]{2,1,0:T(8,128)(2,1)S(1)} %get-tuple-element.176), channel_id=1, source_target_pairs={{0,1},{2,3},{4,5},{6,7},{8,9},{10,11},{12,13},{14,15},{16,17},{18,... | collective-permute-start | bytes 38408 | tf_op jit(solution)/shard_map/ppermute | solution.py:15
  21.9 1.3 collective-permute-start.5
  23.2 2.2 collective-permute-start.2
  25.9 1.6 collective-permute-done.5
  32.4 1.6 convert_reduce_fusion
  33.9 1.0 convolution_dynamic-update-slice_fusion.7
  34.9 1.0 convolution_dynamic-update-slice_fusion.6
  35.9 1.0 convolution_dynamic-update-slice_fusion.5
  36.9 1.0 convolution_dynamic-update-slice_fusion.4
  38.9 1.0 convolution_dynamic-update-slice_fusion.3
  39.9 1.0 convolution_dynamic-update-slice_fusion.2
  40.9 1.0 convolution_dynamic-update-slice_fusion.1
  42.4 1.6 convolution_add_fusion.13
  44.0 10.7 %scatter-add.45 = f32[50,50,128]{2,1,0:T(8,128)S(1)} dynamic-update-slice(f32[50,50,128]{2,1,0:T(8,128)S(1)} %scatter-add.44, f32[48,48,128]{2,1,0:T(8,128)S(1)} %convolution_add_fusion.13, s32[]{:T(128)} %bitcast.28, s32[]{:T(128)} %bitcast.29, s32[]{:T(128)} %constant.375.clone.1) | dynamic-update-slice | bytes 2359300 | tf_op jit(solution)/shard_map/scatter-add | solution.py:55
  54.7 2.2 add_select_fusion
  56.9 10.7 %scatter-add.46 = f32[50,50,128]{2,1,0:T(8,128)S(1)} dynamic-update-slice(f32[50,50,128]{2,1,0:T(8,128)S(1)} %scatter-add.45, f32[48,48,128]{2,1,0:T(8,128)S(1)} %add_select_fusion, s32[]{:T(128)} %bitcast.31, s32[]{:T(128)} %bitcast.32, s32[]{:T(128)} %constant.375.clone.1) | dynamic-update-slice | bytes 2359300 | tf_op jit(solution)/shard_map/scatter-add | solution.py:55
  68.2 9.3 %scatter-add.50 = f32[50,50,128]{2,1,0:T(8,128)S(1)} dynamic-update-slice(f32[50,50,128]{2,1,0:T(8,128)S(1)} %fusion.3, f32[48,48,128]{2,1,0:T(8,128)S(1)} %convolution_add_fusion.11, s32[]{:T(128)} %constant.376.clone.1, s32[]{:T(128)} %constant.376.clone.1, s32[]{:T(128)} %constant.375.clone.1) | dynamic-update-slice | bytes 2359300 | tf_op jit(solution)/shard_map/scatter-add | solution.py:55
  77.8 9.3 %scatter-add.51 = f32[50,50,128]{2,1,0:T(8,128)S(1)} dynamic-update-slice(f32[50,50,128]{2,1,0:T(8,128)S(1)} %scatter-add.50, f32[48,48,128]{2,1,0:T(8,128)S(1)} %convolution_add_fusion.10, s32[]{:T(128)} %constant.376.clone.1, s32[]{:T(128)} %constant.379.clone.1, s32[]{:T(128)} %constant.375.clone.1) | dynamic-update-slice | bytes 2359300 | tf_op jit(solution)/shard_map/scatter-add | solution.py:55
  87.8 9.2 %scatter-add.55 = f32[50,50,128]{2,1,0:T(8,128)S(1)} dynamic-update-slice(f32[50,50,128]{2,1,0:T(8,128)S(1)} %fusion.2, f32[48,48,128]{2,1,0:T(8,128)S(1)} %convolution_add_fusion.8, s32[]{:T(128)} %constant.379.clone.1, s32[]{:T(128)} %constant.376.clone.1, s32[]{:T(128)} %constant.375.clone.1) | dynamic-update-slice | bytes 2359300 | tf_op jit(solution)/shard_map/scatter-add | solution.py:55
  97.2 9.2 %scatter-add.56 = f32[50,50,128]{2,1,0:T(8,128)S(1)} dynamic-update-slice(f32[50,50,128]{2,1,0:T(8,128)S(1)} %scatter-add.55, f32[48,48,128]{2,1,0:T(8,128)S(1)} %convolution_add_fusion.7, s32[]{:T(128)} %constant.379.clone.1, s32[]{:T(128)} %constant.379.clone.1, s32[]{:T(128)} %constant.375.clone.1) | dynamic-update-slice | bytes 2359300 | tf_op jit(solution)/shard_map/scatter-add | solution.py:55
  106.4 4.5 %collective-permute-start.6 = (bf16[1,50,128]{2,1,0:T(8,128)(2,1)S(1)}, bf16[1,50,128]{2,1,0:T(8,128)(2,1)S(1)}, u32[]{:S(2)}, u32[]{:S(2)}) collective-permute-start(bf16[1,50,128]{2,1,0:T(8,128)(2,1)S(1)} %get-tuple-element.162), channel_id=1, source_target_pairs={{0,1},{2,3},{4,5},{6,7},{8,9},{10,11},{12,13},{14,15},{16,17},{18,... | collective-permute-start | bytes 38408 | tf_op jit(solution)/shard_map/ppermute | solution.py:15
  111.0 1.5 collective-permute-start.7
  112.4 2.2 collective-permute-start.8
  114.6 2.1 convolution_dynamic-update-slice_fusion
  117.7 40.7 %psum.15 = f32[1,128]{1,0:T(1,128)S(1)} all-reduce(f32[1,128]{1,0:T(1,128)S(1)} %bitcast.199), channel_id=1, replica_groups=mesh['lon'=16,'lat'=2] {'lon','lat'}, use_global_device_ids=true, to_apply=%region_3.4 | all-reduce | flops 128 | bytes 1024 | tf_op jit(solution)/shard_map/psum | solution.py:81
  158.7 4.4 %collective-permute-start.11 = (bf16[48,1,128]{2,1,0:T(2,128)(2,1)S(1)}, bf16[48,1,128]{2,1,0:T(2,128)(2,1)S(1)}, u32[]{:S(2)}, u32[]{:S(2)}) collective-permute-start(bf16[48,1,128]{2,1,0:T(2,128)(2,1)S(1)} %get-tuple-element.172), channel_id=1, source_target_pairs={{2,0},{4,2},{6,4},{8,6},{10,8},{12,10},{14,12},{16,14},{18,16},{20... | collective-permute-start | bytes 36872 | tf_op jit(solution)/shard_map/ppermute | solution.py:17
  163.7 1.0 collective-permute-done.10
  166.1 77.9 %all-reduce.3.cloned.1.call-done = f32[1152,128]{1,0:T(8,128)} async-done(((f32[1152,128]{1,0:T(8,128)}), f32[1152,128]{1,0:T(8,128)}) %all-reduce.3.cloned.1.call-update) | async-done | bytes 589840 | tf_op jit(solution)/shard_map/psum | solution.py:81
  244.0 1.9 broadcast_multiply_fusion
  (68 shorter events, 15.2 us)
Async XLA Ops:
  7.2 8.7 %copy-start.3 = (s32[3]{0:T(128)S(1)}, s32[3]{0:T(128)}, u32[]{:S(2)}) copy-start(s32[3]{0:T(128)} %constant.381.clone.1) | copy-start | bytes 40
  7.2 10.0 %copy-start = (bf16[48,48,128]{2,1,0:T(8,128)(2,1)S(1)}, bf16[48,48,128]{2,1,0:T(8,128)(2,1)}, u32[]{:S(2)}) copy-start(bf16[48,48,128]{2,1,0:T(8,128)(2,1)} %param.30) | copy-start | bytes 1769476
  7.2 236.9 %all-reduce.3.cloned.1.call-start = ((), (), s32[]{:S(2)}) async-start(), calls=%async_computation | async-start | bytes 1179648 | tf_op jit(solution)/shard_map/psum | solution.py:81
  8.3 8.9 %collective-permute-start = (bf16[48,1,128]{2,1,0:T(2,128)(2,1)S(1)}, bf16[48,1,128]{2,1,0:T(2,128)(2,1)S(1)}, u32[]{:S(2)}, u32[]{:S(2)}) collective-permute-start(bf16[48,1,128]{2,1,0:T(2,128)(2,1)S(1)} %get-tuple-element.179), channel_id=1, source_target_pairs={{0,2},{2,4},{4,6},{6,8},{8,10},{10,12},{12,14},{14,16},{16,18},{18... | collective-permute-start | bytes 36872 | tf_op jit(solution)/shard_map/ppermute | solution.py:15
  8.8 8.4 %collective-permute-start.1 = (bf16[48,1,128]{2,1,0:T(2,128)(2,1)S(1)}, bf16[48,1,128]{2,1,0:T(2,128)(2,1)S(1)}, u32[]{:S(2)}, u32[]{:S(2)}) collective-permute-start(bf16[48,1,128]{2,1,0:T(2,128)(2,1)S(1)} %get-tuple-element.180), channel_id=1, source_target_pairs={{2,0},{4,2},{6,4},{8,6},{10,8},{12,10},{14,12},{16,14},{18,16},{20... | collective-permute-start | bytes 36872 | tf_op jit(solution)/shard_map/ppermute | solution.py:17
  17.2 10.7 %collective-permute-start.3 = (bf16[1,50,128]{2,1,0:T(8,128)(2,1)S(1)}, bf16[1,50,128]{2,1,0:T(8,128)(2,1)S(1)}, u32[]{:S(2)}, u32[]{:S(2)}) collective-permute-start(bf16[1,50,128]{2,1,0:T(8,128)(2,1)S(1)} %get-tuple-element.176), channel_id=1, source_target_pairs={{0,1},{2,3},{4,5},{6,7},{8,9},{10,11},{12,13},{14,15},{16,17},{18,... | collective-permute-start | bytes 38408 | tf_op jit(solution)/shard_map/ppermute | solution.py:15
  21.0 4.9 %collective-permute-start.4 = (bf16[50,128]{1,0:T(8,128)(2,1)S(1)}, bf16[50,128]{1,0:T(8,128)(2,1)S(1)}, u32[]{:S(2)}, u32[]{:S(2)}) collective-permute-start(bf16[50,128]{1,0:T(8,128)(2,1)S(1)} %bitcast.196), channel_id=1, source_target_pairs={{0,16},{2,18},{4,20},{6,22},{8,24},{10,26},{12,28},{14,30},{16,0},... | collective-permute-start | bytes 38408 | tf_op jit(solution)/shard_map/ppermute | solution.py:27
  21.9 5.6 %collective-permute-start.5 = (bf16[1,50,128]{2,1,0:T(8,128)(2,1)S(1)}, bf16[1,50,128]{2,1,0:T(8,128)(2,1)S(1)}, u32[]{:S(2)}, u32[]{:S(2)}) collective-permute-start(bf16[1,50,128]{2,1,0:T(8,128)(2,1)S(1)} %get-tuple-element.175), channel_id=1, source_target_pairs={{1,0},{3,2},{5,4},{7,6},{9,8},{11,10},{13,12},{15,14},{17,16},{19,... | collective-permute-start | bytes 38408 | tf_op jit(solution)/shard_map/ppermute | solution.py:17
  23.2 4.7 %collective-permute-start.2 = (bf16[50,128]{1,0:T(8,128)(2,1)S(1)}, bf16[50,128]{1,0:T(8,128)(2,1)S(1)}, u32[]{:S(2)}, u32[]{:S(2)}) collective-permute-start(bf16[50,128]{1,0:T(8,128)(2,1)S(1)} %bitcast.197), channel_id=1, source_target_pairs={{0,16},{2,18},{4,20},{6,22},{8,24},{10,26},{12,28},{14,30},{16,0},... | collective-permute-start | bytes 38408 | tf_op jit(solution)/shard_map/ppermute | solution.py:27
  28.4 1.0 copy-start.2
  29.1 2.6 %copy-start.1 = (bf16[48,48,128]{2,1,0:T(8,128)(2,1)}, bf16[48,48,128]{2,1,0:T(8,128)(2,1)S(1)}, u32[]{:S(2)}) copy-start(bf16[48,48,128]{2,1,0:T(8,128)(2,1)S(1)} %get-tuple-element.165) | copy-start | bytes 1769476
  29.1 0.7 copy-start.4
  31.3 1.1 copy-start.5
  106.4 52.0 %collective-permute-start.6 = (bf16[1,50,128]{2,1,0:T(8,128)(2,1)S(1)}, bf16[1,50,128]{2,1,0:T(8,128)(2,1)S(1)}, u32[]{:S(2)}, u32[]{:S(2)}) collective-permute-start(bf16[1,50,128]{2,1,0:T(8,128)(2,1)S(1)} %get-tuple-element.162), channel_id=1, source_target_pairs={{0,1},{2,3},{4,5},{6,7},{8,9},{10,11},{12,13},{14,15},{16,17},{18,... | collective-permute-start | bytes 38408 | tf_op jit(solution)/shard_map/ppermute | solution.py:15
  111.0 47.5 %collective-permute-start.7 = (bf16[1,50,128]{2,1,0:T(8,128)(2,1)S(1)}, bf16[1,50,128]{2,1,0:T(8,128)(2,1)S(1)}, u32[]{:S(2)}, u32[]{:S(2)}) collective-permute-start(bf16[1,50,128]{2,1,0:T(8,128)(2,1)S(1)} %get-tuple-element.163), channel_id=1, source_target_pairs={{1,0},{3,2},{5,4},{7,6},{9,8},{11,10},{13,12},{15,14},{17,16},{19,... | collective-permute-start | bytes 38408 | tf_op jit(solution)/shard_map/ppermute | solution.py:17
  112.4 46.0 %collective-permute-start.8 = (bf16[50,128]{1,0:T(8,128)(2,1)S(1)}, bf16[50,128]{1,0:T(8,128)(2,1)S(1)}, u32[]{:S(2)}, u32[]{:S(2)}) collective-permute-start(bf16[50,128]{1,0:T(8,128)(2,1)S(1)} %bitcast.195), channel_id=1, source_target_pairs={{0,16},{2,18},{4,20},{6,22},{8,24},{10,26},{12,28},{14,30},{16,0},... | collective-permute-start | bytes 38408 | tf_op jit(solution)/shard_map/ppermute | solution.py:27
  116.8 41.6 %collective-permute-start.9 = (bf16[50,128]{1,0:T(8,128)(2,1)S(1)}, bf16[50,128]{1,0:T(8,128)(2,1)S(1)}, u32[]{:S(2)}, u32[]{:S(2)}) collective-permute-start(bf16[50,128]{1,0:T(8,128)(2,1)S(1)} %bitcast.194), channel_id=1, source_target_pairs={{0,16},{2,18},{4,20},{6,22},{8,24},{10,26},{12,28},{14,30},{16,0},... | collective-permute-start | bytes 38408 | tf_op jit(solution)/shard_map/ppermute | solution.py:27
  158.6 6.1 %collective-permute-start.10 = (bf16[48,1,128]{2,1,0:T(2,128)(2,1)S(1)}, bf16[48,1,128]{2,1,0:T(2,128)(2,1)S(1)}, u32[]{:S(2)}, u32[]{:S(2)}) collective-permute-start(bf16[48,1,128]{2,1,0:T(2,128)(2,1)S(1)} %get-tuple-element.171), channel_id=1, source_target_pairs={{0,2},{2,4},{4,6},{6,8},{8,10},{10,12},{12,14},{14,16},{16,18},{18... | collective-permute-start | bytes 36872 | tf_op jit(solution)/shard_map/ppermute | solution.py:15
  158.7 6.0 %collective-permute-start.11 = (bf16[48,1,128]{2,1,0:T(2,128)(2,1)S(1)}, bf16[48,1,128]{2,1,0:T(2,128)(2,1)S(1)}, u32[]{:S(2)}, u32[]{:S(2)}) collective-permute-start(bf16[48,1,128]{2,1,0:T(2,128)(2,1)S(1)} %get-tuple-element.172), channel_id=1, source_target_pairs={{2,0},{4,2},{6,4},{8,6},{10,8},{12,10},{14,12},{16,14},{18,16},{20... | collective-permute-start | bytes 36872 | tf_op jit(solution)/shard_map/ppermute | solution.py:17
Sparse Core Ops, SparseCore 0:
  116.9 127.0 all-reduce.2
where the time goes:
time: 253 us
  waiting for transfers between devices  80.9 us (32%)
  local copies, waits for them, and re-layouts  62.9 us (25%)
  blocking collectives  40.7 us (16%)
  starting transfers between devices  27.3 us (11%)
  matrix products  21.1 us (8%)
  between operations  14.4 us (6%)
  other arithmetic  5.49 us (2%)
    psum x1, waiting for transfers between devices, shards(): kernel_sum, bias_sum = lax.psum((kernel_terms, bias_terms), ('lon', 'lat'))  77.9 us
    scatter-add x7, local copies, waits for them, and re-layouts, shards(): padded_grad.at[tap_a:tap_a + rows, tap_b:tap_b + cols]  58.3 us
    psum x1, blocking collectives, shards(): kernel_sum, bias_sum = lax.psum((kernel_terms, bias_terms), ('lon', 'lat'))  40.7 us
    ppermute x4, starting transfers between devices, extended(): lax.ppermute(head, axis, [((i + 1) % count, i) for i in range(ends)])  12.2 us
    dot_general x9, matrix products, shards(): lax.dot_general(window, pre_grad, (((0,), (0,)), ((), ())), preferred_ele...  10.1 us
    ppermute x4, starting transfers between devices, extended(): lax.ppermute(tail, axis, [(i, (i + 1) % count) for i in range(ends)])  8.93 us
    ppermute x4, starting transfers between devices, from_behind(): return lax.ppermute(value, axis, pairs)  6.11 us
    dot_general x9, matrix products, shards(): jnp.dot(pre_grad, weight[tap_a, tap_b].T, preferred_element_type=jnp.floa...  6 us
  transfers between devices with their start and end apart: 13, of which 4 were waited for; matrix products, arithmetic and copies ran while one was open for 3% of the time, Pallas kernels for 0%

commit v1 on v0

v1 whole, which is shorter than its diff:
```python
import functools
import math

import jax
import jax.numpy as jnp
from jax import lax
from jax.experimental import pallas as pl
from jax.experimental.pallas import tpu as pltpu
from jax.sharding import PartitionSpec as P

MESH = pl.DeviceIdType.MESH
F32 = jnp.float32
BF16 = jnp.bfloat16
CHUNK = 8
EXTRA = 16


def kernel(
    lons, lats, x_ref, w_ref, b_ref, c_ref,
    out_ref, gin_ref, wg_ref, bg_ref,
    xc, pc, pg, hrows, hcols, hcorn, hc32, scol32, scol, dwt, bacc,
    sbuf, r1, s2, r2, gath,
    ssem, rsem, s1sem, r1sem, s2sem, r2sem, s3sem, r3sem,
):
    rows, cols, ch = x_ref.shape
    lon, lat = lax.axis_index("lon"), lax.axis_index("lat")
    half = lons // 2
    gl, gt = math.gcd(lons, 4), math.gcd(lats, 2)
    n1 = gl * gt
    n2 = (lons // gl) * (lats // gt)
    part = 9 * ch // n1

    top, bottom = lat == 0, lat == lats - 1
    n_lat = jnp.where(top, lat, lat - 1)
    s_lat = jnp.where(bottom, lat, lat + 1)
    n_lon = jnp.where(top, lon + half, lon)
    s_lon = jnp.where(bottom, lon + half, lon)

    def at(lon_at, lat_at):
        return (lax.rem(lon_at + lons, lons), lat_at)

    north, south = at(n_lon, n_lat), at(s_lon, s_lat)
    west, east = at(lon - 1, lat), at(lon + 1, lat)
    nw, ne = at(n_lon - 1, n_lat), at(n_lon + 1, n_lat)
    sw, se = at(s_lon - 1, s_lat), at(s_lon + 1, s_lat)

    g1 = lax.rem(lon, gl) * gt + lax.rem(lat, gt)
    g2 = (lon // gl) * (lats // gt) + lat // gt

    def peer1(k):
        q = lax.rem(g1 + k, n1)
        return q, ((lon // gl) * gl + q // gt, (lat // gt) * gt + lax.rem(q, gt))

    def peer2(k):
        q = lax.rem(g2 + k, n2)
        wide = lats // gt
        return q, ((q // wide) * gl + lax.rem(lon, gl), lax.rem(q, wide) * gt + lax.rem(lat, gt))

    barrier = pltpu.get_barrier_semaphore()
    greeted = [north, south, west, east, nw, ne, sw, se]
    greeted += [peer1(k)[1] for k in range(1, n1)] + [peer2(k)[1] for k in range(1, n2)]
    for device in greeted:
        pl.semaphore_signal(barrier, inc=1, device_id=device, device_id_type=MESH)

    def stage_columns(turn, src):
        def body(i, carry):
            for k in range(4):
                r = i * 4 + k
                scol32[0, pl.ds(r, 1), :] = src[r, 0:16, :].astype(F32)[0:1]
                scol32[1, pl.ds(r, 1), :] = src[r, cols - 16 : cols, :].astype(F32)[15:16]
            return carry

        lax.fori_loop(0, rows // 4, body, 0)
        scol[turn] = scol32[...].astype(BF16)

    def halo_copies(turn, src):
        lo, hi = slice(0, 16), slice(cols - 16, cols)
        to_north = jnp.where(top, 0, 1)
        to_south = jnp.where(bottom, 1, 0)
        to_nw, to_ne = jnp.where(top, 1, 3), jnp.where(top, 0, 2)
        to_sw, to_se = jnp.where(bottom, 3, 1), jnp.where(bottom, 2, 0)
        plan = [
            (scol.at[turn, 1], hcols.at[turn, 0], 2, east),
            (scol.at[turn, 0], hcols.at[turn, 1], 3, west),
            (src.at[0], hrows.at[turn, to_north], to_north, north),
            (src.at[rows - 1], hrows.at[turn, to_south], to_south, south),
            (src.at[0, lo, :], hcorn.at[turn, to_nw], 4 + to_nw, nw),
            (src.at[0, hi, :], hcorn.at[turn, to_ne], 4 + to_ne, ne),
            (src.at[rows - 1, lo, :], hcorn.at[turn, to_sw], 4 + to_sw, sw),
            (src.at[rows - 1, hi, :], hcorn.at[turn, to_se], 4 + to_se, se),
        ]
        return [
            pltpu.make_async_remote_copy(
                src_ref=s, dst_ref=d, send_sem=ssem.at[turn, i], recv_sem=rsem.at[turn, sem],
                device_id=device, device_id_type=MESH,
            )
            for i, (s, d, sem, device) in enumerate(plan)
        ]

    def halo_wait(turn):
        slots = [hrows.at[turn, 0], hrows.at[turn, 1], hcols.at[turn, 0], hcols.at[turn, 1]]
        slots += [hcorn.at[turn, i] for i in range(4)]
        for i, slot in enumerate(slots):
            pltpu.make_async_remote_copy(
                src_ref=slot, dst_ref=slot, send_sem=ssem.at[turn, i], recv_sem=rsem.at[turn, i],
                device_id=east, device_id_type=MESH,
            ).wait_recv()

    place = lax.broadcasted_iota(jnp.int32, (cols, ch), 0)

    def put_row(dst, at_row, centre, west_cell, east_cell):
        wide = centre.astype(F32)
        before = jnp.where(place == 0, west_cell, pltpu.roll(wide, 1, 0))
        after = jnp.where(place == cols - 1, east_cell, pltpu.roll(wide, cols - 1, 0))
        dst[at_row, :, 0:ch] = before.astype(BF16)
        dst[at_row, :, ch : 2 * ch] = centre
        dst[at_row, :, 2 * ch : 3 * ch] = after.astype(BF16)

    def widen(turn, src, dst):
        hc32[...] = hcols[turn].astype(F32)

        def body(i, carry):
            for k in range(4):
                r = i * 4 + k
                put_row(dst, r + 1, src[r], hc32[0, pl.ds(r, 1), :], hc32[1, pl.ds(r, 1), :])
            return carry

        lax.fori_loop(0, rows // 4, body, 0)
        for side, at_row in ((0, 0), (1, rows + 1)):
            west_cell = hcorn[turn, 2 * side].astype(F32)[15:16]
            east_cell = hcorn[turn, 2 * side + 1].astype(F32)[0:1]
            put_row(dst, at_row, hrows[turn, side], west_cell, east_cell)

    def windows(src, r0):
        return jnp.concatenate(
            [src[pl.ds(r0 + a, CHUNK)].reshape(CHUNK * cols, 3 * ch) for a in range(3)], axis=1
        )

    stage_columns(0, x_ref)
    pl.semaphore_wait(barrier, len(greeted))
    first = halo_copies(0, x_ref)
    for copy in first:
        copy.start()
    dwt[...] = jnp.zeros_like(dwt)
    bacc[...] = jnp.zeros_like(bacc)
    halo_wait(0)
    widen(0, x_ref, xc)

    def forward(i, carry):
        r0 = i * CHUNK
        lhs = windows(xc, r0)
        weight = w_ref[...].reshape(9 * ch, ch)
        pre = jnp.dot(lhs, weight, preferred_element_type=F32) + b_ref[...]
        sig = 1.0 / (1.0 + jnp.exp(-pre))
        out_ref[pl.ds(r0, CHUNK)] = (pre * sig).astype(BF16).reshape(CHUNK, cols, ch)
        cot = c_ref[pl.ds(r0, CHUNK)].reshape(CHUNK * cols, ch).astype(F32)
        grad = (cot * sig * (1.0 + pre * (1.0 - sig))).astype(BF16)
        pg[pl.ds(r0, CHUNK)] = grad.reshape(CHUNK, cols, ch)
        bacc[...] += jnp.sum(grad.astype(F32), axis=0, keepdims=True)
        dwt[...] += lax.dot_general(grad, lhs, (((0,), (0,)), ((), ())), preferred_element_type=F32)
        return carry

    lax.fori_loop(0, rows // CHUNK, forward, 0)

    stage_columns(1, pg)
    second = halo_copies(1, pg)
    for copy in second:
        copy.start()

    line = lax.broadcasted_iota(jnp.int32, (EXTRA, ch), 0)

    def split(total):
        first_part = total.astype(BF16).astype(F32)
        rest = total - first_part
        second_part = rest.astype(BF16).astype(F32)
        third = rest - second_part
        rows_of = jnp.where(line == 0, first_part, jnp.where(line == 1, second_part, jnp.where(line == 2, third, 0.0)))
        return rows_of.astype(BF16)

    for tap in range(9):
        block = dwt[:, tap * ch : (tap + 1) * ch].T.astype(BF16)
        low = tap * ch
        while low < (tap + 1) * ch:
            q = low // part
            high = min((tap + 1) * ch, (q + 1) * part)
            sbuf[q, low - q * part : high - q * part, :] = block[low - tap * ch : high - tap * ch]
            low = high
    bias_rows = split(bacc[...])
    for q in range(n1):
        sbuf[q, part : part + EXTRA, :] = bias_rows

    def copies1():
        result = []
        for k in range(1, n1):
            q, device = peer1(k)
            result.append(
                pltpu.make_async_remote_copy(
                    src_ref=sbuf.at[q], dst_ref=r1.at[g1], send_sem=s1sem.at[k], recv_sem=r1sem.at[g1],
                    device_id=device, device_id_type=MESH,
                )
            )
        return result

    def wait_from(buffer, sems, send_sems, k, q):
        pltpu.make_async_remote_copy(
            src_ref=buffer.at[q], dst_ref=buffer.at[q], send_sem=send_sems.at[k], recv_sem=sems.at[q],
            device_id=east, device_id_type=MESH,
        ).wait_recv()

    sent1 = copies1()
    for copy in sent1:
        copy.start()
    r1[g1] = sbuf[g1]

    halo_wait(1)
    widen(1, pg, pc)

    def kernel_for(taps):
        return jnp.concatenate([w_ref[a, b] for a in taps for b in (2, 1, 0)], axis=1)

    def back(lhs, rhs):
        return lax.dot_general(lhs, rhs, (((1,), (1,)), ((), ())), preferred_element_type=F32)

    def backward(i, carry):
        r0 = i * CHUNK
        grad = back(windows(pc, r0), kernel_for((2, 1, 0)))
        gin_ref[pl.ds(r0, CHUNK)] = grad.astype(BF16).reshape(CHUNK, cols, ch)
        return carry

    lax.fori_loop(0, rows // CHUNK, backward, 0)

    plain = kernel_for((2, 1, 0))
    lhs = jnp.concatenate([pc[a] for a in range(3)], axis=1)
    gin_ref[0] = back(lhs, jnp.where(top, kernel_for((0, 1, 0)), plain)).astype(BF16)
    lhs = jnp.concatenate([pc[rows - 1 + a] for a in range(3)], axis=1)
    gin_ref[rows - 1] = back(lhs, jnp.where(bottom, kernel_for((2, 1, 2)), plain)).astype(BF16)

    for k in range(1, n1):
        wait_from(r1, r1sem, s1sem, k, peer1(k)[0])

    def added(buffer, count):
        total = buffer[0].astype(F32)
        for q in range(1, count):
            total = total + buffer[q].astype(F32)
        return total[:part], jnp.sum(total[part:], axis=0, keepdims=True)

    block, bias_sum = added(r1, n1)
    s2[0:part, :] = block.astype(BF16)
    s2[part : part + EXTRA, :] = split(bias_sum)
    sent2 = []
    for k in range(1, n2):
        q, device = peer2(k)
        sent2.append(
            pltpu.make_async_remote_copy(
                src_ref=s2, dst_ref=r2.at[g2], send_sem=s2sem.at[k], recv_sem=r2sem.at[g2],
                device_id=device, device_id_type=MESH,
            )
        )
    for copy in sent2:
        copy.start()
    r2[g2] = s2[...]
    for k in range(1, n2):
        wait_from(r2, r2sem, s2sem, k, peer2(k)[0])
    block, bias_sum = added(r2, n2)
    scale = 1.0 / math.sqrt(rows * cols * lons * lats)
    bg_ref[...] = bias_sum * scale
    gath[g1] = (block * scale).astype(BF16)
    sent3 = []
    for k in range(1, n1):
        q, device = peer1(k)
        sent3.append(
            pltpu.make_async_remote_copy(
                src_ref=gath.at[g1], dst_ref=gath.at[g1], send_sem=s3sem.at[k], recv_sem=r3sem.at[g1],
                device_id=device, device_id_type=MESH,
            )
        )
    for copy in sent3:
        copy.start()
    for k in range(1, n1):
        wait_from(gath, r3sem, s3sem, k, peer1(k)[0])
    for q in range(n1):
        wg_ref[q] = gath[q].astype(F32)
    for copy in first + second + sent1 + sent2 + sent3:
        copy.wait_send()


def shards(lons, lats, inputs, weight, bias, cotangent):
    rows, cols, ch = inputs.shape
    gl, gt = math.gcd(lons, 4), math.gcd(lats, 2)
    n1 = gl * gt
    n2 = (lons // gl) * (lats // gt)
    part = 9 * ch // n1
    vmem = pl.BlockSpec(memory_space=pltpu.VMEM)
    dma = pltpu.SemaphoreType.DMA
    outputs, input_grad, weight_grad, bias_grad = pl.pallas_call(
        functools.partial(kernel, lons, lats),
        out_shape=(
            jax.ShapeDtypeStruct((rows, cols, ch), BF16),
            jax.ShapeDtypeStruct((rows, cols, ch), BF16),
            jax.ShapeDtypeStruct((n1, part, ch), F32),
            jax.ShapeDtypeStruct((1, ch), F32),
        ),
        in_specs=[vmem] * 4,
        out_specs=(vmem,) * 4,
        scratch_shapes=[
            pltpu.VMEM((rows + 2, cols, 3 * ch), BF16),
            pltpu.VMEM((rows + 2, cols, 3 * ch), BF16),
            pltpu.VMEM((rows, cols, ch), BF16),
            pltpu.VMEM((2, 2, cols, ch), BF16),
            pltpu.VMEM((2, 2, rows, ch), BF16),
            pltpu.VMEM((2, 4, 16, ch), BF16),
            pltpu.VMEM((2, rows, ch), F32),
            pltpu.VMEM((2, rows, ch), F32),
            pltpu.VMEM((2, 2, rows, ch), BF16),
            pltpu.VMEM((ch, 9 * ch), F32),
            pltpu.VMEM((1, ch), F32),
            pltpu.VMEM((n1, part + EXTRA, ch), BF16),
            pltpu.VMEM((n1, part + EXTRA, ch), BF16),
            pltpu.VMEM((part + EXTRA, ch), BF16),
            pltpu.VMEM((n2, part + EXTRA, ch), BF16),
            pltpu.VMEM((n1, part, ch), BF16),
            dma((2, 8)),
            dma((2, 8)),
            dma((n1,)),
            dma((n1,)),
            dma((n2,)),
            dma((n2,)),
            dma((n1,)),
            dma((n1,)),
        ],
        compiler_params=pltpu.CompilerParams(
            collective_id=0, has_side_effects=True, vmem_limit_bytes=48 * 1024 * 1024
        ),
        name="conv_silu_grads",
    )(inputs, weight, bias.reshape(1, ch), cotangent)
    return outputs, input_grad, weight_grad.reshape(3, 3, ch, ch), bias_grad.reshape(ch)


def solution(mesh):
    lons, lats = mesh.shape["lon"], mesh.shape["lat"]
    in_specs = (P("lat", "lon", None), P(), P(), P("lat", "lon", None))
    out_specs = (P("lat", "lon", None), P("lat", "lon", None), P(), P())
    return jax.shard_map(
        functools.partial(shards, lons, lats), mesh=mesh, in_specs=in_specs, out_specs=out_specs, check_vma=False
    )
```

time: 253 us -> 40.4 us (0.16)
  waiting for transfers between devices: 80.9 us -> 0 us
  local copies, waits for them, and re-layouts: 62.9 us -> 6.69 us
  blocking collectives: 40.7 us -> 0 us
  Pallas kernels: 0 us -> 32.8 us
  starting transfers between devices: 27.3 us -> 0 us
  matrix products: 21.1 us -> 0 us
  between operations: 14.4 us -> 0.65 us
  other arithmetic: 5.49 us -> 0 us
    psum x1 -> x0, waiting for transfers between devices: 77.9 us -> none  [shards(): kernel_sum, bias_sum = lax.psum((kernel_terms, bias_terms), ('lon', 'lat'))]
    scatter-add x9 -> x0, local copies, waits for them, and re-layouts: 58.6 us -> none  [the longest x7 58.3 us: shards(): padded_grad.at[tap_a:tap_a + rows, tap_b:tap_b + cols]]
    psum x1 -> x0, blocking collectives: 40.7 us -> none  [shards(): kernel_sum, bias_sum = lax.psum((kernel_terms, bias_terms), ('lon', 'lat'))]
    pallas_call x0 -> x1, Pallas kernels: none -> 32.8 us  [shards(): pl.pallas_call(functools.partial(kernel, lons, lats), out_shape=(jax.Shap...]
    ppermute x12 -> x0, starting transfers between devices: 27.3 us -> none  [the longest x4 12.2 us: extended(): lax.ppermute(head, axis, [((i + 1) % count, i) for i in range(ends)])]
    dot_general x27 -> x0, matrix products: 21.1 us -> none  [the longest x9 10.1 us: shards(): lax.dot_general(window, pre_grad, (((0,), (0,)), ((), ())), preferred_ele...]
    unnamed x12, local copies, waits for them, and re-layouts: 1.17 us -> 6.69 us
    ppermute x12 -> x0, waiting for transfers between devices: 2.97 us -> none  [the longest x4 1.59 us: extended(): lax.ppermute(head, axis, [((i + 1) % count, i) for i in range(ends)])]
  transfers between devices with their start and end apart: 13 -> 0, of which waited for: 4 -> 0; matrix products, arithmetic and copies ran while one was open for 3% -> 0% of each run, Pallas kernels for 0% -> 0%
where the time goes in v1:
time: 40.4 us; the launch traced here: 40.2 us
  Pallas kernels  32.8 us (81%)
  local copies, waits for them, and re-layouts  6.69 us (17%)
  between operations  0.65 us (2%)
    pallas_call x1, Pallas kernels, shards(): pl.pallas_call(functools.partial(kernel, lons, lats), out_shape=(jax.Shap...  32.8 us
    unnamed x12, local copies, waits for them, and re-layouts  6.69 us

profile of v1, /device:TPU:0, one launch (start us, length us, event | category | flops | bytes accessed | tf_op | source)
XLA Modules:
  0.0 40.2 jit_solution(15959216251806158688)
XLA Ops:
  0.6 0.0 copy-start.3
  0.6 0.6 %copy-done.3 = f32[128]{0:T(128)S(1)} copy-done((f32[128]{0:T(128)S(1)}, f32[128]{0:T(128)}, u32[]{:S(2)}) %copy-start.3) | copy-done | bytes 536
  1.3 0.0 copy-start
  1.3 1.1 %copy-done = bf16[48,48,128]{2,1,0:T(8,128)(2,1)S(1)} copy-done((bf16[48,48,128]{2,1,0:T(8,128)(2,1)S(1)}, bf16[48,48,128]{2,1,0:T(8,128)(2,1)}, u32[]{:S(2)}) %copy-start) | copy-done | bytes 589848
  2.4 0.0 copy-start.1
  2.4 1.1 %copy-done.1 = bf16[48,48,128]{2,1,0:T(8,128)(2,1)S(1)} copy-done((bf16[48,48,128]{2,1,0:T(8,128)(2,1)S(1)}, bf16[48,48,128]{2,1,0:T(8,128)(2,1)}, u32[]{:S(2)}) %copy-start.1) | copy-done | bytes 589848
  3.4 0.0 copy-start.2
  3.4 1.0 %copy-done.2 = bf16[3,3,128,128]{3,2,1,0:T(8,128)(2,1)S(1)} copy-done((bf16[3,3,128,128]{3,2,1,0:T(8,128)(2,1)S(1)}, bf16[3,3,128,128]{3,2,1,0:T(8,128)(2,1)}, u32[]{:S(2)}) %copy-start.2) | copy-done | bytes 294936
  4.4 32.8 %conv_silu_grads.1 = (bf16[48,48,128]{2,1,0:T(8,128)(2,1)S(1)}, bf16[48,48,128]{2,1,0:T(8,128)(2,1)S(1)}, f32[8,144,128]{2,1,0:T(8,128)S(1)}, f32[1,128]{1,0:T(1,128)S(1)}) custom-call(bf16[48,48,128]{2,1,0:T(8,128)(2,1)S(1)} %copy-done, bf16[3,3,128,128]{3,2,1,0:T(8,128)(2,1)S(1)} %copy-done.2, f32[1,128]{1,0:T(1,128)S(1)} %bitcast.4, ...), custom_call_target="tpu_custom_call" | custom-call | tf_op jit(solution)/shard_map/conv_silu_grads/pallas_call | solution.py:295
  37.2 0.8 %copy.12 = bf16[48,48,128]{2,1,0:T(8,128)(2,1)} copy(bf16[48,48,128]{2,1,0:T(8,128)(2,1)S(1)} %get-tuple-element.16) | data formatting | bytes 1179648
  38.0 0.8 %copy.13 = bf16[48,48,128]{2,1,0:T(8,128)(2,1)} copy(bf16[48,48,128]{2,1,0:T(8,128)(2,1)S(1)} %get-tuple-element.17) | data formatting | bytes 1179648
  38.8 0.8 %copy.14 = f32[3,3,128,128]{3,2,1,0:T(8,128)} copy(f32[3,3,128,128]{3,2,1,0:T(8,128)S(1)} %bitcast.3) | data formatting | bytes 1179648
  39.6 0.5 %copy.15 = f32[128]{0:T(128)} copy(f32[128]{0:T(128)S(1)} %bitcast.5) | data formatting | bytes 1024
Async XLA Ops:
  0.6 0.7 %copy-start.3 = (f32[128]{0:T(128)S(1)}, f32[128]{0:T(128)}, u32[]{:S(2)}) copy-start(f32[128]{0:T(128)} %param.6) | copy-start | bytes 1540
  1.3 1.1 %copy-start = (bf16[48,48,128]{2,1,0:T(8,128)(2,1)S(1)}, bf16[48,48,128]{2,1,0:T(8,128)(2,1)}, u32[]{:S(2)}) copy-start(bf16[48,48,128]{2,1,0:T(8,128)(2,1)} %x_ref.1) | copy-start | bytes 1769476
  2.4 1.1 %copy-start.1 = (bf16[48,48,128]{2,1,0:T(8,128)(2,1)S(1)}, bf16[48,48,128]{2,1,0:T(8,128)(2,1)}, u32[]{:S(2)}) copy-start(bf16[48,48,128]{2,1,0:T(8,128)(2,1)} %c_ref.1) | copy-start | bytes 1769476
  3.4 1.0 %copy-start.2 = (bf16[3,3,128,128]{3,2,1,0:T(8,128)(2,1)S(1)}, bf16[3,3,128,128]{3,2,1,0:T(8,128)(2,1)}, u32[]{:S(2)}) copy-start(bf16[3,3,128,128]{3,2,1,0:T(8,128)(2,1)} %w_ref.1) | copy-start | bytes 884740

commit v2 on v1

--- a/solution.py
+++ b/solution.py
@@ -16,19 +16,24 @@
 
 
 def kernel(
-    lons, lats, x_ref, w_ref, b_ref, c_ref,
+    lons, lats, x_hbm, w_hbm, b_hbm, c_hbm,
     out_ref, gin_ref, wg_ref, bg_ref,
-    xc, pc, pg, hrows, hcols, hcorn, hc32, scol32, scol, dwt, bacc,
+    x_ref, w_ref, b_ref, c_ref,
+    xc, pc, pg, pgt, hrows, hcols, hcorn, hc32, scol32, scol, bacc,
     sbuf, r1, s2, r2, gath,
-    ssem, rsem, s1sem, r1sem, s2sem, r2sem, s3sem, r3sem,
+    lsem, ssem, rsem, s1sem, r1sem, s2sem, r2sem, s3sem, r3sem,
 ):
+    pairs = ((x_hbm, x_ref), (w_hbm, w_ref), (b_hbm, b_ref), (c_hbm, c_ref))
+    loads = [pltpu.make_async_copy(src, dst, lsem.at[i]) for i, (src, dst) in enumerate(pairs)]
+    for load in loads:
+        load.start()
     rows, cols, ch = x_ref.shape
     lon, lat = lax.axis_index("lon"), lax.axis_index("lat")
     half = lons // 2
     gl, gt = math.gcd(lons, 4), math.gcd(lats, 2)
     n1 = gl * gt
     n2 = (lons // gl) * (lats // gt)
-    part = 9 * ch // n1
+    part = 3 * ch // n1
 
     top, bottom = lat == 0, lat == lats - 1
     n_lat = jnp.where(top, lat, lat - 1)
@@ -136,13 +141,15 @@
             [src[pl.ds(r0 + a, CHUNK)].reshape(CHUNK * cols, 3 * ch) for a in range(3)], axis=1
         )
 
+    loads[0].wait()
     stage_columns(0, x_ref)
     pl.semaphore_wait(barrier, len(greeted))
     first = halo_copies(0, x_ref)
     for copy in first:
         copy.start()
-    dwt[...] = jnp.zeros_like(dwt)
     bacc[...] = jnp.zeros_like(bacc)
+    for load in loads[1:]:
+        load.wait()
     halo_wait(0)
     widen(0, x_ref, xc)
 
@@ -157,7 +164,7 @@
         grad = (cot * sig * (1.0 + pre * (1.0 - sig))).astype(BF16)
         pg[pl.ds(r0, CHUNK)] = grad.reshape(CHUNK, cols, ch)
         bacc[...] += jnp.sum(grad.astype(F32), axis=0, keepdims=True)
-        dwt[...] += lax.dot_general(grad, lhs, (((0,), (0,)), ((), ())), preferred_element_type=F32)
+        pgt[:, pl.ds(pl.multiple_of(r0 * cols, ch), CHUNK * cols)] = grad.T
         return carry
 
     lax.fori_loop(0, rows // CHUNK, forward, 0)
@@ -177,40 +184,80 @@
         rows_of = jnp.where(line == 0, first_part, jnp.where(line == 1, second_part, jnp.where(line == 2, third, 0.0)))
         return rows_of.astype(BF16)
 
-    for tap in range(9):
-        block = dwt[:, tap * ch : (tap + 1) * ch].T.astype(BF16)
-        low = tap * ch
-        while low < (tap + 1) * ch:
-            q = low // part
-            high = min((tap + 1) * ch, (q + 1) * part)
-            sbuf[q, low - q * part : high - q * part, :] = block[low - tap * ch : high - tap * ch]
-            low = high
-    bias_rows = split(bacc[...])
-    for q in range(n1):
-        sbuf[q, part : part + EXTRA, :] = bias_rows
-
-    def copies1():
-        result = []
+    def lines(a):
+        return part + EXTRA if a == 0 else part
+
+    def wait_from(buffer, a, sems, send_sems, k, q):
+        slot = buffer.at[a, q, 0 : lines(a)]
+        pltpu.make_async_remote_copy(
+            src_ref=slot, dst_ref=slot, send_sem=send_sems.at[a, k], recv_sem=sems.at[a, q],
+            device_id=east, device_id_type=MESH,
+        ).wait_recv()
+
+    sent = []
+
+    def send(src, dst, send_sem, recv_sem, device):
+        copy = pltpu.make_async_remote_copy(
+            src_ref=src, dst_ref=dst, send_sem=send_sem, recv_sem=recv_sem, device_id=device, device_id_type=MESH,
+        )
+        copy.start()
+        sent.append(copy)
+
+    def third(a):
+        window = xc[a : a + rows].reshape(rows * cols, 3 * ch)
+        grad = jnp.dot(pgt[...], window, preferred_element_type=F32)
+        for b in range(3):
+            block = grad[:, b * ch : (b + 1) * ch].T.astype(BF16)
+            low = b * ch
+            while low < (b + 1) * ch:
+                q = low // part
+                high = min((b + 1) * ch, (q + 1) * part)
+                sbuf[a, q, low - q * part : high - q * part, :] = block[low - b * ch : high - b * ch]
+                low = high
+        if a == 0:
+            bias_rows = split(bacc[...])
+            for q in range(n1):
+                sbuf[0, q, part : part + EXTRA, :] = bias_rows
+        size = slice(0, lines(a))
         for k in range(1, n1):
             q, device = peer1(k)
-            result.append(
-                pltpu.make_async_remote_copy(
-                    src_ref=sbuf.at[q], dst_ref=r1.at[g1], send_sem=s1sem.at[k], recv_sem=r1sem.at[g1],
-                    device_id=device, device_id_type=MESH,
-                )
-            )
-        return result
-
-    def wait_from(buffer, sems, send_sems, k, q):
-        pltpu.make_async_remote_copy(
-            src_ref=buffer.at[q], dst_ref=buffer.at[q], send_sem=send_sems.at[k], recv_sem=sems.at[q],
-            device_id=east, device_id_type=MESH,
-        ).wait_recv()
-
-    sent1 = copies1()
-    for copy in sent1:
-        copy.start()
-    r1[g1] = sbuf[g1]
+            send(sbuf.at[a, q, size], r1.at[a, g1, size], s1sem.at[a, k], r1sem.at[a, g1], device)
+        r1[a, g1, size, :] = sbuf[a, g1, size, :]
+
+    def added(buffer, a, count):
+        total = buffer[a, 0, 0 : lines(a), :].astype(F32)
+        for q in range(1, count):
+            total = total + buffer[a, q, 0 : lines(a), :].astype(F32)
+        return total
+
+    def along(a):
+        for k in range(1, n1):
+            wait_from(r1, a, r1sem, s1sem, k, peer1(k)[0])
+        total = added(r1, a, n1)
+        s2[a, 0:part, :] = total[:part].astype(BF16)
+        if a == 0:
+            s2[a, part : part + EXTRA, :] = split(jnp.sum(total[part:], axis=0, keepdims=True))
+        size = slice(0, lines(a))
+        for k in range(1, n2):
+            q, device = peer2(k)
+            send(s2.at[a, size], r2.at[a, g2, size], s2sem.at[a, k], r2sem.at[a, g2], device)
+        r2[a, g2, size, :] = s2[a, size, :]
+
+    scale = 1.0 / math.sqrt(rows * cols * lons * lats)
+
+    def around(a):
+        for k in range(1, n2):
+            wait_from(r2, a, r2sem, s2sem, k, peer2(k)[0])
+        total = added(r2, a, n2)
+        if a == 0:
+            bg_ref[...] = jnp.sum(total[part:], axis=0, keepdims=True) * scale
+        gath[a, g1] = (total[:part] * scale).astype(BF16)
+        for k in range(1, n1):
+            q, device = peer1(k)
+            send(gath.at[a, g1], gath.at[a, g1], s3sem.at[a, k], r3sem.at[a, g1], device)
+
+    for a in range(3):
+        third(a)
 
     halo_wait(1)
     widen(1, pg, pc)
@@ -227,7 +274,15 @@
         gin_ref[pl.ds(r0, CHUNK)] = grad.astype(BF16).reshape(CHUNK, cols, ch)
         return carry
 
-    lax.fori_loop(0, rows // CHUNK, backward, 0)
+    steps = rows // CHUNK
+    lax.fori_loop(0, steps // 3, backward, 0)
+    along(0)
+    lax.fori_loop(steps // 3, 2 * steps // 3, backward, 0)
+    along(1)
+    around(0)
+    lax.fori_loop(2 * steps // 3, steps, backward, 0)
+    along(2)
+    around(1)
 
     plain = kernel_for((2, 1, 0))
     lhs = jnp.concatenate([pc[a] for a in range(3)], axis=1)
@@ -235,53 +290,32 @@
     lhs = jnp.concatenate([pc[rows - 1 + a] for a in range(3)], axis=1)
     gin_ref[rows - 1] = back(lhs, jnp.where(bottom, kernel_for((2, 1, 2)), plain)).astype(BF16)
 
-    for k in range(1, n1):
-        wait_from(r1, r1sem, s1sem, k, peer1(k)[0])
-
-    def added(buffer, count):
-        total = buffer[0].astype(F32)
-        for q in range(1, count):
-            total = total + buffer[q].astype(F32)
-        return total[:part], jnp.sum(total[part:], axis=0, keepdims=True)
-
-    block, bias_sum = added(r1, n1)
-    s2[0:part, :] = block.astype(BF16)
-    s2[part : part + EXTRA, :] = split(bias_sum)
-    sent2 = []
-    for k in range(1, n2):
-        q, device = peer2(k)
-        sent2.append(
+    around(2)
+    for a in range(3):
+        for k in range(1, n1):
+            q = peer1(k)[0]
             pltpu.make_async_remote_copy(
-                src_ref=s2, dst_ref=r2.at[g2], send_sem=s2sem.at[k], recv_sem=r2sem.at[g2],
-                device_id=device, device_id_type=MESH,
-            )
-        )
-    for copy in sent2:
+                src_ref=gath.at[a, q], dst_ref=gath.at[a, q], send_sem=s3sem.at[a, k], recv_sem=r3sem.at[a, q],
+                device_id=east, device_id_type=MESH,
+            ).wait_recv()
+    wg_ref[...] = gath[...]
+    for copy in first + second + sent:
+        copy.wait_send()
+
+
+def store(out_v, gin_v, wg_v, bg_v, out_hbm, gin_hbm, wg_hbm, bg_hbm, wide, sems):
+    copies = [
+        pltpu.make_async_copy(out_v, out_hbm, sems.at[0]),
+        pltpu.make_async_copy(gin_v, gin_hbm, sems.at[1]),
+        pltpu.make_async_copy(bg_v, bg_hbm, sems.at[2]),
+        pltpu.make_async_copy(wide, wg_hbm, sems.at[3]),
+    ]
+    for copy in copies[:3]:
         copy.start()
-    r2[g2] = s2[...]
-    for k in range(1, n2):
-        wait_from(r2, r2sem, s2sem, k, peer2(k)[0])
-    block, bias_sum = added(r2, n2)
-    scale = 1.0 / math.sqrt(rows * cols * lons * lats)
-    bg_ref[...] = bias_sum * scale
-    gath[g1] = (block * scale).astype(BF16)
-    sent3 = []
-    for k in range(1, n1):
-        q, device = peer1(k)
-        sent3.append(
-            pltpu.make_async_remote_copy(
-                src_ref=gath.at[g1], dst_ref=gath.at[g1], send_sem=s3sem.at[k], recv_sem=r3sem.at[g1],
-                device_id=device, device_id_type=MESH,
-            )
-        )
-    for copy in sent3:
-        copy.start()
-    for k in range(1, n1):
-        wait_from(gath, r3sem, s3sem, k, peer1(k)[0])
-    for q in range(n1):
-        wg_ref[q] = gath[q].astype(F32)
-    for copy in first + second + sent1 + sent2 + sent3:
-        copy.wait_send()
+    wide[...] = wg_v[...].astype(F32)
+    copies[3].start()
+    for copy in copies:
+        copy.wait()
 
 
 def shards(lons, lats, inputs, weight, bias, cotangent):
@@ -289,50 +323,70 @@
     gl, gt = math.gcd(lons, 4), math.gcd(lats, 2)
     n1 = gl * gt
     n2 = (lons // gl) * (lats // gt)
-    part = 9 * ch // n1
+    part = 3 * ch // n1
     vmem = pl.BlockSpec(memory_space=pltpu.VMEM)
     dma = pltpu.SemaphoreType.DMA
-    outputs, input_grad, weight_grad, bias_grad = pl.pallas_call(
+    anywhere = pl.BlockSpec(memory_space=pltpu.HBM)
+    results = pl.pallas_call(
         functools.partial(kernel, lons, lats),
         out_shape=(
             jax.ShapeDtypeStruct((rows, cols, ch), BF16),
             jax.ShapeDtypeStruct((rows, cols, ch), BF16),
-            jax.ShapeDtypeStruct((n1, part, ch), F32),
+            jax.ShapeDtypeStruct((3, n1, part, ch), BF16),
             jax.ShapeDtypeStruct((1, ch), F32),
         ),
-        in_specs=[vmem] * 4,
+        in_specs=[anywhere] * 4,
         out_specs=(vmem,) * 4,
         scratch_shapes=[
+            pltpu.VMEM((rows, cols, ch), BF16),
+            pltpu.VMEM((3, 3, ch, ch), BF16),
+            pltpu.VMEM((1, ch), F32),
+            pltpu.VMEM((rows, cols, ch), BF16),
             pltpu.VMEM((rows + 2, cols, 3 * ch), BF16),
             pltpu.VMEM((rows + 2, cols, 3 * ch), BF16),
             pltpu.VMEM((rows, cols, ch), BF16),
+            pltpu.VMEM((ch, rows * cols), BF16),
             pltpu.VMEM((2, 2, cols, ch), BF16),
             pltpu.VMEM((2, 2, rows, ch), BF16),
             pltpu.VMEM((2, 4, 16, ch), BF16),
             pltpu.VMEM((2, rows, ch), F32),
             pltpu.VMEM((2, rows, ch), F32),
             pltpu.VMEM((2, 2, rows, ch), BF16),
-            pltpu.VMEM((ch, 9 * ch), F32),
             pltpu.VMEM((1, ch), F32),
-            pltpu.VMEM((n1, part + EXTRA, ch), BF16),
-            pltpu.VMEM((n1, part + EXTRA, ch), BF16),
-            pltpu.VMEM((part + EXTRA, ch), BF16),
-            pltpu.VMEM((n2, part + EXTRA, ch), BF16),
-            pltpu.VMEM((n1, part, ch), BF16),
+            pltpu.VMEM((3, n1, part + EXTRA, ch), BF16),
+            pltpu.VMEM((3, n1, part + EXTRA, ch), BF16),
+            pltpu.VMEM((3, part + EXTRA, ch), BF16),
+            pltpu.VMEM((3, n2, part + EXTRA, ch), BF16),
+            pltpu.VMEM((3, n1, part, ch), BF16),
+            dma((4,)),
             dma((2, 8)),
             dma((2, 8)),
-            dma((n1,)),
-            dma((n1,)),
-            dma((n2,)),
-            dma((n2,)),
-            dma((n1,)),
-            dma((n1,)),
+            dma((3, n1)),
+            dma((3, n1)),
+            dma((3, n2)),
+            dma((3, n2)),
+            dma((3, n1)),
+            dma((3, n1)),
         ],
         compiler_params=pltpu.CompilerParams(
-            collective_id=0, has_side_effects=True, vmem_limit_bytes=48 * 1024 * 1024
+            collective_id=0, has_side_effects=True, vmem_limit_bytes=53 * 1024 * 1024
         ),
         name="conv_silu_grads",
     )(inputs, weight, bias.reshape(1, ch), cotangent)
+    outputs, input_grad, weight_grad, bias_grad = pl.pallas_call(
+        store,
+        out_shape=(
+            jax.ShapeDtypeStruct((rows, cols, ch), BF16),
+            jax.ShapeDtypeStruct((rows, cols, ch), BF16),
+            jax.ShapeDtypeStruct((3, n1, part, ch), F32),
+            jax.ShapeDtypeStruct((1, ch), F32),
+        ),
+        in_specs=[vmem] * 4,
+        out_specs=(anywhere,) * 4,
+        scratch_shapes=[pltpu.VMEM((3, n1, part, ch), F32), dma((4,))],
+        compiler_params=pltpu.CompilerParams(vmem_limit_bytes=48 * 1024 * 1024),
+        name="write_results",
+    )(*results)
     return outputs, input_grad, weight_grad.reshape(3, 3, ch, ch), bias_grad.reshape(ch)
 
 

time: 40.4 us -> 39.4 us (0.975)
  local copies, waits for them, and re-layouts: 6.69 us -> 3.73 us
  Pallas kernels: 32.8 us -> 34.7 us
    unnamed x12 -> x8, local copies, waits for them, and re-layouts: 6.69 us -> 3.73 us
    pallas_call x0 -> x1, Pallas kernels: none -> 1.24 us  [shards(): pl.pallas_call(store, out_shape=(jax.ShapeDtypeStruct((rows, cols, ch), B...]
    pallas_call x1, Pallas kernels: 32.8 us -> 33.5 us  [shards(): pl.pallas_call(functools.partial(kernel, lons, lats), out_shape=(jax.Shap...]
where the time goes in v2:
time: 39.4 us; the launch traced here: 39.1 us
  Pallas kernels  34.7 us (88%)
  local copies, waits for them, and re-layouts  3.73 us (9%)
  between operations  0.66 us (2%)
    pallas_call x1, Pallas kernels, shards(): pl.pallas_call(functools.partial(kernel, lons, lats), out_shape=(jax.Shap...  33.5 us
    unnamed x8, local copies, waits for them, and re-layouts  3.73 us
    pallas_call x1, Pallas kernels, shards(): pl.pallas_call(store, out_shape=(jax.ShapeDtypeStruct((rows, cols, ch), B...  1.24 us

profile of v2, /device:TPU:0, one launch (start us, length us, event | category | flops | bytes accessed | tf_op | source)
XLA Modules:
  0.0 39.1 jit_solution(15840106080904528326)
XLA Ops:
  0.6 0.0 copy-start.3
  0.6 0.6 %copy-done.3 = f32[128]{0:T(128)S(1)} copy-done((f32[128]{0:T(128)S(1)}, f32[128]{0:T(128)}, u32[]{:S(2)}) %copy-start.3) | copy-done | bytes 536
  1.3 0.0 copy-start.2
  1.3 1.0 %copy-done.2 = bf16[3,3,128,128]{3,2,1,0:T(8,128)(2,1)S(1)} copy-done((bf16[3,3,128,128]{3,2,1,0:T(8,128)(2,1)S(1)}, bf16[3,3,128,128]{3,2,1,0:T(8,128)(2,1)}, u32[]{:S(2)}) %copy-start.2) | copy-done | bytes 294936
  2.2 33.5 %conv_silu_grads.1 = (bf16[48,48,128]{2,1,0:T(8,128)(2,1)}, bf16[48,48,128]{2,1,0:T(8,128)(2,1)}, bf16[3,8,48,128]{3,2,1,0:T(8,128)(2,1)S(1)}, f32[1,128]{1,0:T(1,128)S(1)}) custom-call(bf16[48,48,128]{2,1,0:T(8,128)(2,1)} %x_hbm.1, bf16[3,3,128,128]{3,2,1,0:T(8,128)(2,1)S(1)} %copy-done.2, f32[1,128]{1,0:T(1,128)S(1)} %bitcast.3, bf16[48,48,128]{2,1,0:T(8,128)(2,1)} %c_hbm.1), custom_call_target="tpu_custom_call" | custom-call | tf_op jit(solution)/shard_map/conv_silu_grads/pallas_call | solution.py:330
  35.8 0.0 copy-start
  35.8 1.1 %copy-done = bf16[48,48,128]{2,1,0:T(8,128)(2,1)S(1)} copy-done((bf16[48,48,128]{2,1,0:T(8,128)(2,1)S(1)}, bf16[48,48,128]{2,1,0:T(8,128)(2,1)}, u32[]{:S(2)}) %copy-start) | copy-done | bytes 589848
  36.8 0.0 copy-start.1
  36.8 1.1 %copy-done.1 = bf16[48,48,128]{2,1,0:T(8,128)(2,1)S(1)} copy-done((bf16[48,48,128]{2,1,0:T(8,128)(2,1)S(1)}, bf16[48,48,128]{2,1,0:T(8,128)(2,1)}, u32[]{:S(2)}) %copy-start.1) | copy-done | bytes 589848
  37.9 1.2 %write_results.1 = (bf16[48,48,128]{2,1,0:T(8,128)(2,1)}, bf16[48,48,128]{2,1,0:T(8,128)(2,1)}, f32[3,8,48,128]{3,2,1,0:T(8,128)}, f32[1,128]{1,0:T(1,128)}) custom-call(bf16[48,48,128]{2,1,0:T(8,128)(2,1)S(1)} %copy-done, bf16[48,48,128]{2,1,0:T(8,128)(2,1)S(1)} %copy-done.1, bf16[3,8,48,128]{3,2,1,0:T(8,128)(2,1)S(1)} %get-tuple-element.14.wg_v, ...), custom_call_target="tpu_custom_call" | custom-call | tf_op jit(solution)/shard_map/write_results/pallas_call | solution.py:376
Async XLA Ops:
  0.6 0.7 %copy-start.3 = (f32[128]{0:T(128)S(1)}, f32[128]{0:T(128)}, u32[]{:S(2)}) copy-start(f32[128]{0:T(128)} %param.6) | copy-start | bytes 1540
  1.3 1.0 %copy-start.2 = (bf16[3,3,128,128]{3,2,1,0:T(8,128)(2,1)S(1)}, bf16[3,3,128,128]{3,2,1,0:T(8,128)(2,1)}, u32[]{:S(2)}) copy-start(bf16[3,3,128,128]{3,2,1,0:T(8,128)(2,1)} %w_hbm.1) | copy-start | bytes 884740
  35.8 1.1 %copy-start = (bf16[48,48,128]{2,1,0:T(8,128)(2,1)S(1)}, bf16[48,48,128]{2,1,0:T(8,128)(2,1)}, u32[]{:S(2)}) copy-start(bf16[48,48,128]{2,1,0:T(8,128)(2,1)} %get-tuple-element.12.out_v) | copy-start | bytes 1769476
  36.8 1.1 %copy-start.1 = (bf16[48,48,128]{2,1,0:T(8,128)(2,1)S(1)}, bf16[48,48,128]{2,1,0:T(8,128)(2,1)}, u32[]{:S(2)}) copy-start(bf16[48,48,128]{2,1,0:T(8,128)(2,1)} %get-tuple-element.13.gin_v) | copy-start | bytes 1769476

commit v3 on v2

--- a/solution.py
+++ b/solution.py
@@ -11,17 +11,17 @@
 MESH = pl.DeviceIdType.MESH
 F32 = jnp.float32
 BF16 = jnp.bfloat16
-CHUNK = 8
+CHUNK = 16
 EXTRA = 16
 
 
 def kernel(
     lons, lats, x_hbm, w_hbm, b_hbm, c_hbm,
-    out_ref, gin_ref, wg_ref, bg_ref,
-    x_ref, w_ref, b_ref, c_ref,
-    xc, pc, pg, pgt, hrows, hcols, hcorn, hc32, scol32, scol, bacc,
+    out_hbm, gin_hbm, wg_hbm, bg_hbm,
+    x_ref, w_ref, b_ref, c_ref, out_ref, gin_ref, wg_ref, bg_ref,
+    vt, xc, pc, pg, pgt, hrows, hcols, hcorn, hc32, scol32, scol, bacc,
     sbuf, r1, s2, r2, gath,
-    lsem, ssem, rsem, s1sem, r1sem, s2sem, r2sem, s3sem, r3sem,
+    lsem, osem, ssem, rsem, s1sem, r1sem, s2sem, r2sem, s3sem, r3sem,
 ):
     pairs = ((x_hbm, x_ref), (w_hbm, w_ref), (b_hbm, b_ref), (c_hbm, c_ref))
     loads = [pltpu.make_async_copy(src, dst, lsem.at[i]) for i, (src, dst) in enumerate(pairs)]
@@ -150,6 +150,16 @@
     bacc[...] = jnp.zeros_like(bacc)
     for load in loads[1:]:
         load.wait()
+    for a in range(3):
+        for b in range(3):
+            vt[(3 * a + b) * ch : (3 * a + b + 1) * ch, :] = w_ref[2 - a, 2 - b].T
+    stores = []
+
+    def store(src, dst):
+        copy = pltpu.make_async_copy(src, dst, osem.at[len(stores)])
+        copy.start()
+        stores.append(copy)
+
     halo_wait(0)
     widen(0, x_ref, xc)
 
@@ -158,7 +168,7 @@
         lhs = windows(xc, r0)
         weight = w_ref[...].reshape(9 * ch, ch)
         pre = jnp.dot(lhs, weight, preferred_element_type=F32) + b_ref[...]
-        sig = 1.0 / (1.0 + jnp.exp(-pre))
+        sig = 0.5 * jnp.tanh(0.5 * pre) + 0.5
         out_ref[pl.ds(r0, CHUNK)] = (pre * sig).astype(BF16).reshape(CHUNK, cols, ch)
         cot = c_ref[pl.ds(r0, CHUNK)].reshape(CHUNK * cols, ch).astype(F32)
         grad = (cot * sig * (1.0 + pre * (1.0 - sig))).astype(BF16)
@@ -169,6 +179,7 @@
 
     lax.fori_loop(0, rows // CHUNK, forward, 0)
 
+    store(out_ref, out_hbm)
     stage_columns(1, pg)
     second = halo_copies(1, pg)
     for copy in second:
@@ -251,6 +262,7 @@
         total = added(r2, a, n2)
         if a == 0:
             bg_ref[...] = jnp.sum(total[part:], axis=0, keepdims=True) * scale
+            store(bg_ref, bg_hbm)
         gath[a, g1] = (total[:part] * scale).astype(BF16)
         for k in range(1, n1):
             q, device = peer1(k)
@@ -262,15 +274,9 @@
     halo_wait(1)
     widen(1, pg, pc)
 
-    def kernel_for(taps):
-        return jnp.concatenate([w_ref[a, b] for a in taps for b in (2, 1, 0)], axis=1)
-
-    def back(lhs, rhs):
-        return lax.dot_general(lhs, rhs, (((1,), (1,)), ((), ())), preferred_element_type=F32)
-
     def backward(i, carry):
         r0 = i * CHUNK
-        grad = back(windows(pc, r0), kernel_for((2, 1, 0)))
+        grad = jnp.dot(windows(pc, r0), vt[...], preferred_element_type=F32)
         gin_ref[pl.ds(r0, CHUNK)] = grad.astype(BF16).reshape(CHUNK, cols, ch)
         return carry
 
@@ -284,11 +290,15 @@
     along(2)
     around(1)
 
-    plain = kernel_for((2, 1, 0))
-    lhs = jnp.concatenate([pc[a] for a in range(3)], axis=1)
-    gin_ref[0] = back(lhs, jnp.where(top, kernel_for((0, 1, 0)), plain)).astype(BF16)
-    lhs = jnp.concatenate([pc[rows - 1 + a] for a in range(3)], axis=1)
-    gin_ref[rows - 1] = back(lhs, jnp.where(bottom, kernel_for((2, 1, 2)), plain)).astype(BF16)
+    def row_of(at_row, rhs):
+        lhs = jnp.concatenate([pc[at_row + a] for a in range(3)], axis=1)
+        gin_ref[at_row] = jnp.dot(lhs, rhs, preferred_element_type=F32).astype(BF16)
+
+    third_of = 3 * ch
+    near, far = vt[0:third_of, :], vt[2 * third_of :, :]
+    row_of(0, jnp.concatenate([jnp.where(top, far, near), vt[third_of:, :]], axis=0))
+    row_of(rows - 1, jnp.concatenate([vt[: 2 * third_of, :], jnp.where(bottom, near, far)], axis=0))
+    store(gin_ref, gin_hbm)
 
     around(2)
     for a in range(3):
@@ -298,22 +308,20 @@
                 src_ref=gath.at[a, q], dst_ref=gath.at[a, q], send_sem=s3sem.at[a, k], recv_sem=r3sem.at[a, q],
                 device_id=east, device_id_type=MESH,
             ).wait_recv()
-    wg_ref[...] = gath[...]
+        wg_ref[a] = gath[a].astype(F32)
+        store(wg_ref.at[a], wg_hbm.at[a])
     for copy in first + second + sent:
         copy.wait_send()
-
-
-def store(out_v, gin_v, wg_v, bg_v, out_hbm, gin_hbm, wg_hbm, bg_hbm, wide, sems):
-    copies = [
-        pltpu.make_async_copy(out_v, out_hbm, sems.at[0]),
-        pltpu.make_async_copy(gin_v, gin_hbm, sems.at[1]),
-        pltpu.make_async_copy(bg_v, bg_hbm, sems.at[2]),
-        pltpu.make_async_copy(wide, wg_hbm, sems.at[3]),
-    ]
-    for copy in copies[:3]:
+    for copy in stores:
+        copy.wait()
+
+
+def store_all(*refs):
+    sems = refs[-1]
+    count = len(refs) // 2
+    copies = [pltpu.make_async_copy(refs[i], refs[count + i], sems.at[i]) for i in range(count)]
+    for copy in copies:
         copy.start()
-    wide[...] = wg_v[...].astype(F32)
-    copies[3].start()
     for copy in copies:
         copy.wait()
 
@@ -324,7 +332,7 @@
     n1 = gl * gt
     n2 = (lons // gl) * (lats // gt)
     part = 3 * ch // n1
-    vmem = pl.BlockSpec(memory_space=pltpu.VMEM)
+    limit = 62 * 1024 * 1024
     dma = pltpu.SemaphoreType.DMA
     anywhere = pl.BlockSpec(memory_space=pltpu.HBM)
     results = pl.pallas_call(
@@ -332,16 +340,21 @@
         out_shape=(
             jax.ShapeDtypeStruct((rows, cols, ch), BF16),
             jax.ShapeDtypeStruct((rows, cols, ch), BF16),
-            jax.ShapeDtypeStruct((3, n1, part, ch), BF16),
+            jax.ShapeDtypeStruct((3, n1, part, ch), F32),
             jax.ShapeDtypeStruct((1, ch), F32),
         ),
         in_specs=[anywhere] * 4,
-        out_specs=(vmem,) * 4,
+        out_specs=(anywhere,) * 4,
         scratch_shapes=[
             pltpu.VMEM((rows, cols, ch), BF16),
             pltpu.VMEM((3, 3, ch, ch), BF16),
             pltpu.VMEM((1, ch), F32),
             pltpu.VMEM((rows, cols, ch), BF16),
+            pltpu.VMEM((rows, cols, ch), BF16),
+            pltpu.VMEM((rows, cols, ch), BF16),
+            pltpu.VMEM((3, n1, part, ch), F32),
+            pltpu.VMEM((1, ch), F32),
+            pltpu.VMEM((9 * ch, ch), BF16),
             pltpu.VMEM((rows + 2, cols, 3 * ch), BF16),
             pltpu.VMEM((rows + 2, cols, 3 * ch), BF16),
             pltpu.VMEM((rows, cols, ch), BF16),
@@ -359,6 +372,7 @@
             pltpu.VMEM((3, n2, part + EXTRA, ch), BF16),
             pltpu.VMEM((3, n1, part, ch), BF16),
             dma((4,)),
+            dma((6,)),
             dma((2, 8)),
             dma((2, 8)),
             dma((3, n1)),
@@ -369,22 +383,22 @@
             dma((3, n1)),
         ],
         compiler_params=pltpu.CompilerParams(
-            collective_id=0, has_side_effects=True, vmem_limit_bytes=53 * 1024 * 1024
+            collective_id=0, has_side_effects=True, vmem_limit_bytes=limit
         ),
         name="conv_silu_grads",
     )(inputs, weight, bias.reshape(1, ch), cotangent)
     outputs, input_grad, weight_grad, bias_grad = pl.pallas_call(
-        store,
+        store_all,
         out_shape=(
             jax.ShapeDtypeStruct((rows, cols, ch), BF16),
             jax.ShapeDtypeStruct((rows, cols, ch), BF16),
             jax.ShapeDtypeStruct((3, n1, part, ch), F32),
             jax.ShapeDtypeStruct((1, ch), F32),
         ),
-        in_specs=[vmem] * 4,
+        in_specs=[anywhere] * 4,
         out_specs=(anywhere,) * 4,
-        scratch_shapes=[pltpu.VMEM((3, n1, part, ch), F32), dma((4,))],
-        compiler_params=pltpu.CompilerParams(vmem_limit_bytes=48 * 1024 * 1024),
+        scratch_shapes=[dma((4,))],
+        compiler_params=pltpu.CompilerParams(vmem_limit_bytes=limit),
         name="write_results",
     )(*results)
     return outputs, input_grad, weight_grad.reshape(3, 3, ch, ch), bias_grad.reshape(ch)

time: 39.4 us -> 87.9 us (2.23)
  Pallas kernels: 34.7 us -> 87.1 us
  local copies, waits for them, and re-layouts: 3.73 us -> 0 us
    pallas_call x1, Pallas kernels: 1.24 us -> 54.8 us  [shards(): pl.pallas_call(store_all, out_shape=(jax.ShapeDtypeStruct((rows, cols, ch...]
    unnamed x8 -> x0, local copies, waits for them, and re-layouts: 3.73 us -> none
    pallas_call x1, Pallas kernels: 33.5 us -> 32.4 us  [shards(): pl.pallas_call(functools.partial(kernel, lons, lats), out_shape=(jax.Shap...]
where the time goes in v3:
time: 87.9 us; the launch traced here: 87.8 us
  Pallas kernels  87.1 us (99%)
    pallas_call x1, Pallas kernels, shards(): pl.pallas_call(store_all, out_shape=(jax.ShapeDtypeStruct((rows, cols, ch...  54.8 us
    pallas_call x1, Pallas kernels, shards(): pl.pallas_call(functools.partial(kernel, lons, lats), out_shape=(jax.Shap...  32.4 us

profile of v3, /device:TPU:0, one launch (start us, length us, event | category | flops | bytes accessed | tf_op | source)
XLA Modules:
  0.0 87.8 jit_solution(13915153711321395180)
XLA Ops:
  0.6 32.4 %conv_silu_grads.1 = (bf16[48,48,128]{2,1,0:T(8,128)(2,1)}, bf16[48,48,128]{2,1,0:T(8,128)(2,1)}, f32[3,8,48,128]{3,2,1,0:T(8,128)}, f32[1,128]{1,0:T(1,128)}) custom-call(bf16[48,48,128]{2,1,0:T(8,128)(2,1)} %x_hbm.1, bf16[3,3,128,128]{3,2,1,0:T(8,128)(2,1)} %w_hbm.1, f32[1,128]{1,0:T(1,128)} %bitcast.3, bf16[48,48,128]{2,1,0:T(8,128)(2,1)} %c_hbm.1), custom_call_target="tpu_custom_call" | custom-call | tf_op jit(solution)/shard_map/conv_silu_grads/pallas_call | solution.py:338
  33.0 54.8 %write_results.1 = (bf16[48,48,128]{2,1,0:T(8,128)(2,1)}, bf16[48,48,128]{2,1,0:T(8,128)(2,1)}, f32[3,8,48,128]{3,2,1,0:T(8,128)}, f32[1,128]{1,0:T(1,128)}) custom-call(bf16[48,48,128]{2,1,0:T(8,128)(2,1)} %get-tuple-element.12.refs_0_, bf16[48,48,128]{2,1,0:T(8,128)(2,1)} %get-tuple-element.13.refs_1_, f32[3,8,48,128]{3,2,1,0:T(8,128)} %get-tuple-element.14.refs_2_, ...), custom_call_target="tpu_custom_call" | custom-call | tf_op jit(solution)/shard_map/write_results/pallas_call | solution.py:390

commit v4 on v3

--- a/solution.py
+++ b/solution.py
@@ -19,7 +19,7 @@
     lons, lats, x_hbm, w_hbm, b_hbm, c_hbm,
     out_hbm, gin_hbm, wg_hbm, bg_hbm,
     x_ref, w_ref, b_ref, c_ref, out_ref, gin_ref, wg_ref, bg_ref,
-    vt, xc, pc, pg, pgt, hrows, hcols, hcorn, hc32, scol32, scol, bacc,
+    vt, xc, pc, pg, pgt, hrows, hcols, hcorn, hc32, scol32, scol, ecol, fix, bacc,
     sbuf, r1, s2, r2, gath,
     lsem, osem, ssem, rsem, s1sem, r1sem, s2sem, r2sem, s3sem, r3sem,
 ):
@@ -67,7 +67,7 @@
     for device in greeted:
         pl.semaphore_signal(barrier, inc=1, device_id=device, device_id_type=MESH)
 
-    def stage_columns(turn, src):
+    def stage_columns(src):
         def body(i, carry):
             for k in range(4):
                 r = i * 4 + k
@@ -76,7 +76,6 @@
             return carry
 
         lax.fori_loop(0, rows // 4, body, 0)
-        scol[turn] = scol32[...].astype(BF16)
 
     def halo_copies(turn, src):
         lo, hi = slice(0, 16), slice(cols - 16, cols)
@@ -142,17 +141,26 @@
         )
 
     loads[0].wait()
-    stage_columns(0, x_ref)
+    stage_columns(x_ref)
+    scol[0] = scol32[...].astype(BF16)
     pl.semaphore_wait(barrier, len(greeted))
     first = halo_copies(0, x_ref)
     for copy in first:
         copy.start()
+
+    nothing = jnp.zeros((1, ch), F32)
+
+    def widen_alone(i, carry):
+        for k in range(4):
+            put_row(xc, i * 4 + k + 1, x_ref[i * 4 + k], nothing, nothing)
+        return carry
+
+    lax.fori_loop(0, rows // 4, widen_alone, 0)
+    xc[0] = jnp.zeros((cols, 3 * ch), BF16)
+    xc[rows + 1] = jnp.zeros((cols, 3 * ch), BF16)
     bacc[...] = jnp.zeros_like(bacc)
     for load in loads[1:]:
         load.wait()
-    for a in range(3):
-        for b in range(3):
-            vt[(3 * a + b) * ch : (3 * a + b + 1) * ch, :] = w_ref[2 - a, 2 - b].T
     stores = []
 
     def store(src, dst):
@@ -160,30 +168,88 @@
         copy.start()
         stores.append(copy)
 
-    halo_wait(0)
-    widen(0, x_ref, xc)
+    def layer(lhs, cot):
+        pre = jnp.dot(lhs, w_ref[...].reshape(9 * ch, ch), preferred_element_type=F32) + b_ref[...]
+        sig = 0.5 * jnp.tanh(0.5 * pre) + 0.5
+        return pre * sig, cot * sig * (1.0 + pre * (1.0 - sig))
 
     def forward(i, carry):
         r0 = i * CHUNK
-        lhs = windows(xc, r0)
-        weight = w_ref[...].reshape(9 * ch, ch)
-        pre = jnp.dot(lhs, weight, preferred_element_type=F32) + b_ref[...]
-        sig = 0.5 * jnp.tanh(0.5 * pre) + 0.5
-        out_ref[pl.ds(r0, CHUNK)] = (pre * sig).astype(BF16).reshape(CHUNK, cols, ch)
         cot = c_ref[pl.ds(r0, CHUNK)].reshape(CHUNK * cols, ch).astype(F32)
-        grad = (cot * sig * (1.0 + pre * (1.0 - sig))).astype(BF16)
-        pg[pl.ds(r0, CHUNK)] = grad.reshape(CHUNK, cols, ch)
-        bacc[...] += jnp.sum(grad.astype(F32), axis=0, keepdims=True)
-        pgt[:, pl.ds(pl.multiple_of(r0 * cols, ch), CHUNK * cols)] = grad.T
+        value, grad = layer(windows(xc, r0), cot)
+        out_ref[pl.ds(r0, CHUNK)] = value.astype(BF16).reshape(CHUNK, cols, ch)
+        pg[pl.ds(r0, CHUNK)] = grad.astype(BF16).reshape(CHUNK, cols, ch)
         return carry
 
     lax.fori_loop(0, rows // CHUNK, forward, 0)
-
-    store(out_ref, out_hbm)
-    stage_columns(1, pg)
+    for a in range(3):
+        for b in range(3):
+            vt[(3 * a + b) * ch : (3 * a + b + 1) * ch, :] = w_ref[2 - a, 2 - b].T
+    stage_columns(c_ref)
+
+    halo_wait(0)
+    hc32[...] = hcols[0].astype(F32)
+    for side, at_row in ((0, 0), (1, rows + 1)):
+        west_cell = hcorn[0, 2 * side].astype(F32)[15:16]
+        east_cell = hcorn[0, 2 * side + 1].astype(F32)[0:1]
+        put_row(xc, at_row, hrows[0, side], west_cell, east_cell)
+        ecol[0, at_row : at_row + 1, :] = xc[at_row, 0:16, :].astype(F32)[0:1]
+        ecol[1, at_row : at_row + 1, :] = xc[at_row, cols - 16 : cols, :].astype(F32)[15:16]
+    tile = lax.broadcasted_iota(jnp.int32, (16, ch), 0)
+
+    def patch(i, carry):
+        for k in range(4):
+            r = i * 4 + k
+            left, right = hc32[0, pl.ds(r, 1), :], hc32[1, pl.ds(r, 1), :]
+            edge = xc[r + 1, 0:16, :].astype(F32)
+            ecol[0, pl.ds(r + 1, 1), :] = jnp.concatenate([left, edge[0:1, ch:]], axis=1)
+            xc[r + 1, 0:16, 0:ch] = jnp.where(tile == 0, left, edge[:, 0:ch]).astype(BF16)
+            edge = xc[r + 1, cols - 16 : cols, :].astype(F32)
+            ecol[1, pl.ds(r + 1, 1), :] = jnp.concatenate([edge[15:16, : 2 * ch], right], axis=1)
+            xc[r + 1, cols - 16 : cols, 2 * ch :] = jnp.where(tile == 15, right, edge[:, 2 * ch :]).astype(BF16)
+        return carry
+
+    lax.fori_loop(0, rows // 4, patch, 0)
+    lhs = [jnp.concatenate([xc[r + a] for a in range(3)], axis=1) for r in (0, rows - 1)]
+    for side in range(2):
+        lhs.append(jnp.concatenate([ecol[side, a : a + rows, :] for a in range(3)], axis=1).astype(BF16))
+    cot = [c_ref[0].astype(F32), c_ref[rows - 1].astype(F32), scol32[0], scol32[1]]
+    value, grad = layer(jnp.concatenate(lhs, axis=0), jnp.concatenate(cot, axis=0))
+    out_ref[0] = value[0:cols].astype(BF16)
+    out_ref[rows - 1] = value[cols : 2 * cols].astype(BF16)
+    pg[0] = grad[0:cols].astype(BF16)
+    pg[rows - 1] = grad[cols : 2 * cols].astype(BF16)
+    for side in range(2):
+        low = 2 * cols + side * rows
+        fix[0, side] = value[low : low + rows]
+        fix[1, side] = grad[low : low + rows]
+        scol[1, side] = grad[low : low + rows].astype(BF16)
+
+    def put_columns(i, carry):
+        for k in range(4):
+            r = i * 4 + k
+            for which, ref in ((0, out_ref), (1, pg)):
+                for side, start, line_at in ((0, 0, 0), (1, cols - 16, 15)):
+                    old = ref[r, start : start + 16, :].astype(F32)
+                    new = jnp.where(tile == line_at, fix[which, side, pl.ds(r, 1), :], old)
+                    ref[r, start : start + 16, :] = new.astype(BF16)
+        return carry
+
+    lax.fori_loop(0, rows // 4, put_columns, 0)
+
     second = halo_copies(1, pg)
     for copy in second:
         copy.start()
+    store(out_ref, out_hbm)
+
+    def turn_over(i, carry):
+        r0 = i * CHUNK
+        grad = pg[pl.ds(r0, CHUNK)].reshape(CHUNK * cols, ch)
+        bacc[...] += jnp.sum(grad.astype(F32), axis=0, keepdims=True)
+        pgt[:, pl.ds(pl.multiple_of(r0 * cols, ch), CHUNK * cols)] = grad.T
+        return carry
+
+    lax.fori_loop(0, rows // CHUNK, turn_over, 0)
 
     line = lax.broadcasted_iota(jnp.int32, (EXTRA, ch), 0)
 
@@ -317,13 +383,16 @@
 
 
 def store_all(*refs):
-    sems = refs[-1]
-    count = len(refs) // 2
-    copies = [pltpu.make_async_copy(refs[i], refs[count + i], sems.at[i]) for i in range(count)]
-    for copy in copies:
-        copy.start()
-    for copy in copies:
-        copy.wait()
+    sources, targets, staged, sems = refs[0:4], refs[4:8], refs[8:12], refs[12]
+    loads = [pltpu.make_async_copy(s, v, sems.at[0, i]) for i, (s, v) in enumerate(zip(sources, staged))]
+    stores = [pltpu.make_async_copy(v, t, sems.at[1, i]) for i, (v, t) in enumerate(zip(staged, targets))]
+    for load in loads:
+        load.start()
+    for load, save in zip(loads, stores):
+        load.wait()
+        save.start()
+    for save in stores:
+        save.wait()
 
 
 def shards(lons, lats, inputs, weight, bias, cotangent):
@@ -365,6 +434,8 @@
             pltpu.VMEM((2, rows, ch), F32),
             pltpu.VMEM((2, rows, ch), F32),
             pltpu.VMEM((2, 2, rows, ch), BF16),
+            pltpu.VMEM((2, rows + 2, 3 * ch), F32),
+            pltpu.VMEM((2, 2, rows, ch), F32),
             pltpu.VMEM((1, ch), F32),
             pltpu.VMEM((3, n1, part + EXTRA, ch), BF16),
             pltpu.VMEM((3, n1, part + EXTRA, ch), BF16),
@@ -397,7 +468,13 @@
         ),
         in_specs=[anywhere] * 4,
         out_specs=(anywhere,) * 4,
-        scratch_shapes=[dma((4,))],
+        scratch_shapes=[
+            pltpu.VMEM((rows, cols, ch), BF16),
+            pltpu.VMEM((rows, cols, ch), BF16),
+            pltpu.VMEM((3, n1, part, ch), F32),
+            pltpu.VMEM((1, ch), F32),
+            dma((2, 4)),
+        ],
         compiler_params=pltpu.CompilerParams(vmem_limit_bytes=limit),
         name="write_results",
     )(*results)

time: 87.9 us -> 33.3 us (0.38)
  Pallas kernels: 87.1 us -> 32.5 us
    pallas_call x1, Pallas kernels: 54.8 us -> 2.34 us  [shards(): pl.pallas_call(store_all, out_shape=(jax.ShapeDtypeStruct((rows, cols, ch...]
    pallas_call x1, Pallas kernels: 32.4 us -> 30.2 us  [shards(): pl.pallas_call(functools.partial(kernel, lons, lats), out_shape=(jax.Shap...]
where the time goes in v4:
time: 33.3 us; the launch traced here: 33.1 us
  Pallas kernels  32.5 us (98%)
  between operations  0.64 us (2%)
    pallas_call x1, Pallas kernels, shards(): pl.pallas_call(functools.partial(kernel, lons, lats), out_shape=(jax.Shap...  30.2 us
    pallas_call x1, Pallas kernels, shards(): pl.pallas_call(store_all, out_shape=(jax.ShapeDtypeStruct((rows, cols, ch...  2.34 us

profile of v4, /device:TPU:0, one launch (start us, length us, event | category | flops | bytes accessed | tf_op | source)
XLA Modules:
  0.0 33.1 jit_solution(3801115151058712366)
XLA Ops:
  0.6 30.2 %conv_silu_grads.1 = (bf16[48,48,128]{2,1,0:T(8,128)(2,1)}, bf16[48,48,128]{2,1,0:T(8,128)(2,1)}, f32[3,8,48,128]{3,2,1,0:T(8,128)}, f32[1,128]{1,0:T(1,128)}) custom-call(bf16[48,48,128]{2,1,0:T(8,128)(2,1)} %x_hbm.1, bf16[3,3,128,128]{3,2,1,0:T(8,128)(2,1)} %w_hbm.1, f32[1,128]{1,0:T(1,128)} %bitcast.3, bf16[48,48,128]{2,1,0:T(8,128)(2,1)} %c_hbm.1), custom_call_target="tpu_custom_call" | custom-call | tf_op jit(solution)/shard_map/conv_silu_grads/pallas_call | solution.py:407
  30.8 2.3 %write_results.1 = (bf16[48,48,128]{2,1,0:T(8,128)(2,1)}, bf16[48,48,128]{2,1,0:T(8,128)(2,1)}, f32[3,8,48,128]{3,2,1,0:T(8,128)}, f32[1,128]{1,0:T(1,128)}) custom-call(bf16[48,48,128]{2,1,0:T(8,128)(2,1)} %get-tuple-element.12.refs_0_, bf16[48,48,128]{2,1,0:T(8,128)(2,1)} %get-tuple-element.13.refs_1_, f32[3,8,48,128]{3,2,1,0:T(8,128)} %get-tuple-element.14.refs_2_, ...), custom_call_target="tpu_custom_call" | custom-call | tf_op jit(solution)/shard_map/write_results/pallas_call | solution.py:461

commit v5 on v4

--- a/solution.py
+++ b/solution.py
@@ -20,8 +20,8 @@
     out_hbm, gin_hbm, wg_hbm, bg_hbm,
     x_ref, w_ref, b_ref, c_ref, out_ref, gin_ref, wg_ref, bg_ref,
     vt, xc, pc, pg, pgt, hrows, hcols, hcorn, hc32, scol32, scol, ecol, fix, bacc,
-    sbuf, r1, s2, r2, gath,
-    lsem, osem, ssem, rsem, s1sem, r1sem, s2sem, r2sem, s3sem, r3sem,
+    sbuf, r0, s1, r1, s2, r2, gath,
+    lsem, osem, ssem, rsem, gsem,
 ):
     pairs = ((x_hbm, x_ref), (w_hbm, w_ref), (b_hbm, b_ref), (c_hbm, c_ref))
     loads = [pltpu.make_async_copy(src, dst, lsem.at[i]) for i, (src, dst) in enumerate(pairs)]
@@ -31,9 +31,9 @@
     lon, lat = lax.axis_index("lon"), lax.axis_index("lat")
     half = lons // 2
     gl, gt = math.gcd(lons, 4), math.gcd(lats, 2)
-    n1 = gl * gt
+    chips = (gl // 2) * gt
     n2 = (lons // gl) * (lats // gt)
-    part = 3 * ch // n1
+    part = 3 * ch // (2 * chips)
 
     top, bottom = lat == 0, lat == lats - 1
     n_lat = jnp.where(top, lat, lat - 1)
@@ -49,12 +49,14 @@
     nw, ne = at(n_lon - 1, n_lat), at(n_lon + 1, n_lat)
     sw, se = at(s_lon - 1, s_lat), at(s_lon + 1, s_lat)
 
-    g1 = lax.rem(lon, gl) * gt + lax.rem(lat, gt)
+    core = lax.rem(lon, 2)
+    sibling = (lon + 1 - 2 * core, lat)
+    g1 = (lax.rem(lon, gl) // 2) * gt + lax.rem(lat, gt)
     g2 = (lon // gl) * (lats // gt) + lat // gt
 
     def peer1(k):
-        q = lax.rem(g1 + k, n1)
-        return q, ((lon // gl) * gl + q // gt, (lat // gt) * gt + lax.rem(q, gt))
+        q = lax.rem(g1 + k, chips)
+        return q, ((lon // gl) * gl + (q // gt) * 2 + core, (lat // gt) * gt + lax.rem(q, gt))
 
     def peer2(k):
         q = lax.rem(g2 + k, n2)
@@ -63,7 +65,7 @@
 
     barrier = pltpu.get_barrier_semaphore()
     greeted = [north, south, west, east, nw, ne, sw, se]
-    greeted += [peer1(k)[1] for k in range(1, n1)] + [peer2(k)[1] for k in range(1, n2)]
+    greeted += [sibling] + [peer1(k)[1] for k in range(1, chips)] + [peer2(k)[1] for k in range(1, n2)]
     for device in greeted:
         pl.semaphore_signal(barrier, inc=1, device_id=device, device_id_type=MESH)
 
@@ -261,24 +263,26 @@
         rows_of = jnp.where(line == 0, first_part, jnp.where(line == 1, second_part, jnp.where(line == 2, third, 0.0)))
         return rows_of.astype(BF16)
 
-    def lines(a):
-        return part + EXTRA if a == 0 else part
-
-    def wait_from(buffer, a, sems, send_sems, k, q):
-        slot = buffer.at[a, q, 0 : lines(a)]
+    def size(a, count):
+        return slice(0, count + EXTRA if a == 0 else count)
+
+    sent = []
+
+    def send(phase, a, src, dst, device):
         pltpu.make_async_remote_copy(
-            src_ref=slot, dst_ref=slot, send_sem=send_sems.at[a, k], recv_sem=sems.at[a, q],
-            device_id=east, device_id_type=MESH,
-        ).wait_recv()
-
-    sent = []
-
-    def send(src, dst, send_sem, recv_sem, device):
+            src_ref=src, dst_ref=dst, send_sem=gsem.at[0, phase, a], recv_sem=gsem.at[1, phase, a],
+            device_id=device, device_id_type=MESH,
+        ).start()
+
+    def wait_all(phase, a, ref):
         copy = pltpu.make_async_remote_copy(
-            src_ref=src, dst_ref=dst, send_sem=send_sem, recv_sem=recv_sem, device_id=device, device_id_type=MESH,
+            src_ref=ref, dst_ref=ref, send_sem=gsem.at[0, phase, a], recv_sem=gsem.at[1, phase, a],
+            device_id=sibling, device_id_type=MESH,
         )
-        copy.start()
+        copy.wait_recv()
         sent.append(copy)
+
+    half_rows = chips * part
 
     def third(a):
         window = xc[a : a + rows].reshape(rows * cols, 3 * ch)
@@ -287,55 +291,75 @@
             block = grad[:, b * ch : (b + 1) * ch].T.astype(BF16)
             low = b * ch
             while low < (b + 1) * ch:
-                q = low // part
-                high = min((b + 1) * ch, (q + 1) * part)
-                sbuf[a, q, low - q * part : high - q * part, :] = block[low - b * ch : high - b * ch]
+                q = low // half_rows
+                high = min((b + 1) * ch, (q + 1) * half_rows)
+                sbuf[a, q, low - q * half_rows : high - q * half_rows, :] = block[low - b * ch : high - b * ch]
                 low = high
         if a == 0:
             bias_rows = split(bacc[...])
-            for q in range(n1):
-                sbuf[0, q, part : part + EXTRA, :] = bias_rows
-        size = slice(0, lines(a))
-        for k in range(1, n1):
+            for q in range(2):
+                sbuf[0, q, half_rows : half_rows + EXTRA, :] = bias_rows
+        block_size = size(a, half_rows)
+        send(0, a, sbuf.at[a, 1 - core, block_size], r0.at[a, block_size], sibling)
+
+    def plane(a):
+        block_size = size(a, half_rows)
+        wait_all(0, a, r0.at[a, block_size])
+        total = sbuf[a, core, block_size, :].astype(F32) + r0[a, block_size, :].astype(F32)
+        for q in range(chips):
+            s1[a, q, 0:part, :] = total[q * part : (q + 1) * part].astype(BF16)
+        if a == 0:
+            bias_rows = split(jnp.sum(total[half_rows:], axis=0, keepdims=True))
+            for q in range(chips):
+                s1[a, q, part : part + EXTRA, :] = bias_rows
+        for k in range(1, chips):
             q, device = peer1(k)
-            send(sbuf.at[a, q, size], r1.at[a, g1, size], s1sem.at[a, k], r1sem.at[a, g1], device)
-        r1[a, g1, size, :] = sbuf[a, g1, size, :]
+            send(1, a, s1.at[a, q, size(a, part)], r1.at[a, g1, size(a, part)], device)
+        r1[a, g1, size(a, part), :] = s1[a, g1, size(a, part), :]
 
     def added(buffer, a, count):
-        total = buffer[a, 0, 0 : lines(a), :].astype(F32)
+        total = buffer[a, 0, size(a, part), :].astype(F32)
         for q in range(1, count):
-            total = total + buffer[a, q, 0 : lines(a), :].astype(F32)
+            total = total + buffer[a, q, size(a, part), :].astype(F32)
         return total
 
     def along(a):
-        for k in range(1, n1):
-            wait_from(r1, a, r1sem, s1sem, k, peer1(k)[0])
-        total = added(r1, a, n1)
+        wait_all(1, a, r1.at[a, 0 : chips - 1, size(a, part)])
+        total = added(r1, a, chips)
         s2[a, 0:part, :] = total[:part].astype(BF16)
         if a == 0:
             s2[a, part : part + EXTRA, :] = split(jnp.sum(total[part:], axis=0, keepdims=True))
-        size = slice(0, lines(a))
         for k in range(1, n2):
-            q, device = peer2(k)
-            send(s2.at[a, size], r2.at[a, g2, size], s2sem.at[a, k], r2sem.at[a, g2], device)
-        r2[a, g2, size, :] = s2[a, size, :]
+            send(2, a, s2.at[a, size(a, part)], r2.at[a, g2, size(a, part)], peer2(k)[1])
+        r2[a, g2, size(a, part), :] = s2[a, size(a, part), :]
 
     scale = 1.0 / math.sqrt(rows * cols * lons * lats)
 
     def around(a):
-        for k in range(1, n2):
-            wait_from(r2, a, r2sem, s2sem, k, peer2(k)[0])
+        wait_all(2, a, r2.at[a, 0 : n2 - 1, size(a, part)])
         total = added(r2, a, n2)
         if a == 0:
             bg_ref[...] = jnp.sum(total[part:], axis=0, keepdims=True) * scale
             store(bg_ref, bg_hbm)
-        gath[a, g1] = (total[:part] * scale).astype(BF16)
-        for k in range(1, n1):
-            q, device = peer1(k)
-            send(gath.at[a, g1], gath.at[a, g1], s3sem.at[a, k], r3sem.at[a, g1], device)
-
-    for a in range(3):
-        third(a)
+        gath[a, core, g1] = (total[:part] * scale).astype(BF16)
+        for k in range(1, chips):
+            send(3, a, gath.at[a, core, g1], gath.at[a, core, g1], peer1(k)[1])
+
+    def across(a):
+        wait_all(3, a, gath.at[a, core, 0 : chips - 1])
+        send(4, a, gath.at[a, core], gath.at[a, core], sibling)
+        wg_ref[a, core] = gath[a, core].astype(F32)
+
+    def finish(a):
+        wait_all(4, a, gath.at[a, 1 - core])
+        wg_ref[a, 1 - core] = gath[a, 1 - core].astype(F32)
+        store(wg_ref.at[a], wg_hbm.at[a])
+
+    third(0)
+    third(1)
+    plane(0)
+    third(2)
+    plane(1)
 
     halo_wait(1)
     widen(1, pg, pc)
@@ -347,14 +371,16 @@
         return carry
 
     steps = rows // CHUNK
+    plane(2)
+    along(0)
     lax.fori_loop(0, steps // 3, backward, 0)
-    along(0)
+    along(1)
     lax.fori_loop(steps // 3, 2 * steps // 3, backward, 0)
-    along(1)
+    along(2)
     around(0)
     lax.fori_loop(2 * steps // 3, steps, backward, 0)
-    along(2)
     around(1)
+    across(0)
 
     def row_of(at_row, rhs):
         lhs = jnp.concatenate([pc[at_row + a] for a in range(3)], axis=1)
@@ -367,15 +393,11 @@
     store(gin_ref, gin_hbm)
 
     around(2)
-    for a in range(3):
-        for k in range(1, n1):
-            q = peer1(k)[0]
-            pltpu.make_async_remote_copy(
-                src_ref=gath.at[a, q], dst_ref=gath.at[a, q], send_sem=s3sem.at[a, k], recv_sem=r3sem.at[a, q],
-                device_id=east, device_id_type=MESH,
-            ).wait_recv()
-        wg_ref[a] = gath[a].astype(F32)
-        store(wg_ref.at[a], wg_hbm.at[a])
+    across(1)
+    finish(0)
+    across(2)
+    finish(1)
+    finish(2)
     for copy in first + second + sent:
         copy.wait_send()
     for copy in stores:
@@ -398,9 +420,9 @@
 def shards(lons, lats, inputs, weight, bias, cotangent):
     rows, cols, ch = inputs.shape
     gl, gt = math.gcd(lons, 4), math.gcd(lats, 2)
-    n1 = gl * gt
+    chips = (gl // 2) * gt
     n2 = (lons // gl) * (lats // gt)
-    part = 3 * ch // n1
+    part = 3 * ch // (2 * chips)
     limit = 62 * 1024 * 1024
     dma = pltpu.SemaphoreType.DMA
     anywhere = pl.BlockSpec(memory_space=pltpu.HBM)
@@ -409,7 +431,7 @@
         out_shape=(
             jax.ShapeDtypeStruct((rows, cols, ch), BF16),
             jax.ShapeDtypeStruct((rows, cols, ch), BF16),
-            jax.ShapeDtypeStruct((3, n1, part, ch), F32),
+            jax.ShapeDtypeStruct((3, 2, chips, part, ch), F32),
             jax.ShapeDtypeStruct((1, ch), F32),
         ),
         in_specs=[anywhere] * 4,
@@ -421,7 +443,7 @@
             pltpu.VMEM((rows, cols, ch), BF16),
             pltpu.VMEM((rows, cols, ch), BF16),
             pltpu.VMEM((rows, cols, ch), BF16),
-            pltpu.VMEM((3, n1, part, ch), F32),
+            pltpu.VMEM((3, 2, chips, part, ch), F32),
             pltpu.VMEM((1, ch), F32),
             pltpu.VMEM((9 * ch, ch), BF16),
             pltpu.VMEM((rows + 2, cols, 3 * ch), BF16),
@@ -437,21 +459,18 @@
             pltpu.VMEM((2, rows + 2, 3 * ch), F32),
             pltpu.VMEM((2, 2, rows, ch), F32),
             pltpu.VMEM((1, ch), F32),
-            pltpu.VMEM((3, n1, part + EXTRA, ch), BF16),
-            pltpu.VMEM((3, n1, part + EXTRA, ch), BF16),
+            pltpu.VMEM((3, 2, chips * part + EXTRA, ch), BF16),
+            pltpu.VMEM((3, chips * part + EXTRA, ch), BF16),
+            pltpu.VMEM((3, chips, part + EXTRA, ch), BF16),
+            pltpu.VMEM((3, chips, part + EXTRA, ch), BF16),
             pltpu.VMEM((3, part + EXTRA, ch), BF16),
             pltpu.VMEM((3, n2, part + EXTRA, ch), BF16),
-            pltpu.VMEM((3, n1, part, ch), BF16),
+            pltpu.VMEM((3, 2, chips, part, ch), BF16),
             dma((4,)),
             dma((6,)),
             dma((2, 8)),
             dma((2, 8)),
-            dma((3, n1)),
-            dma((3, n1)),
-            dma((3, n2)),
-            dma((3, n2)),
-            dma((3, n1)),
-            dma((3, n1)),
+            dma((2, 5, 3)),
         ],
         compiler_params=pltpu.CompilerParams(
             collective_id=0, has_side_effects=True, vmem_limit_bytes=limit
@@ -463,7 +482,7 @@
         out_shape=(
             jax.ShapeDtypeStruct((rows, cols, ch), BF16),
             jax.ShapeDtypeStruct((rows, cols, ch), BF16),
-            jax.ShapeDtypeStruct((3, n1, part, ch), F32),
+            jax.ShapeDtypeStruct((3, 2, chips, part, ch), F32),
             jax.ShapeDtypeStruct((1, ch), F32),
         ),
         in_specs=[anywhere] * 4,
@@ -471,7 +490,7 @@
         scratch_shapes=[
             pltpu.VMEM((rows, cols, ch), BF16),
             pltpu.VMEM((rows, cols, ch), BF16),
-            pltpu.VMEM((3, n1, part, ch), F32),
+            pltpu.VMEM((3, 2, chips, part, ch), F32),
             pltpu.VMEM((1, ch), F32),
             dma((2, 4)),
         ],

time: 33.3 us -> 32.4 us (0.973)
  the two profiles are of different devices: /device:TPU:0 before, /device:TPU:1 now
where the time goes in v5:
time: 32.4 us; the launch traced here: 32.2 us
  Pallas kernels  31.6 us (98%)
  between operations  0.64 us (2%)
    pallas_call x1, Pallas kernels, shards(): pl.pallas_call(functools.partial(kernel, lons, lats), out_shape=(jax.Shap...  29.3 us
    pallas_call x1, Pallas kernels, shards(): pl.pallas_call(store_all, out_shape=(jax.ShapeDtypeStruct((rows, cols, ch...  2.34 us

profile of v5, /device:TPU:1, one launch (start us, length us, event | category | flops | bytes accessed | tf_op | source)
XLA Modules:
  0.0 32.2 jit_solution(6020670608624710615)
XLA Ops:
  0.6 29.3 %conv_silu_grads.1 = (bf16[48,48,128]{2,1,0:T(8,128)(2,1)}, bf16[48,48,128]{2,1,0:T(8,128)(2,1)}, f32[3,2,4,48,128]{4,3,2,1,0:T(8,128)}, f32[1,128]{1,0:T(1,128)}) custom-call(bf16[48,48,128]{2,1,0:T(8,128)(2,1)} %x_hbm.1, bf16[3,3,128,128]{3,2,1,0:T(8,128)(2,1)} %w_hbm.1, f32[1,128]{1,0:T(1,128)} %bitcast.3, bf16[48,48,128]{2,1,0:T(8,128)(2,1)} %c_hbm.1), custom_call_target="tpu_custom_call" | custom-call | tf_op jit(solution)/shard_map/conv_silu_grads/pallas_call | solution.py:429
  29.9 2.3 %write_results.1 = (bf16[48,48,128]{2,1,0:T(8,128)(2,1)}, bf16[48,48,128]{2,1,0:T(8,128)(2,1)}, f32[3,2,4,48,128]{4,3,2,1,0:T(8,128)}, f32[1,128]{1,0:T(1,128)}) custom-call(bf16[48,48,128]{2,1,0:T(8,128)(2,1)} %get-tuple-element.12.refs_0_, bf16[48,48,128]{2,1,0:T(8,128)(2,1)} %get-tuple-element.13.refs_1_, ...), custom_call_target="tpu_custom_call" | custom-call | tf_op jit(solution)/shard_map/write_results/pallas_call | solution.py:480

commit v6 on v5

--- a/solution.py
+++ b/solution.py
@@ -15,11 +15,15 @@
 EXTRA = 16
 
 
+def padded_cells(rows, cols, ch):
+    return pl.cdiv((rows + 2) * cols, ch) * ch
+
+
 def kernel(
     lons, lats, x_hbm, w_hbm, b_hbm, c_hbm,
     out_hbm, gin_hbm, wg_hbm, bg_hbm,
     x_ref, w_ref, b_ref, c_ref, out_ref, gin_ref, wg_ref, bg_ref,
-    vt, xc, pc, pg, pgt, hrows, hcols, hcorn, hc32, scol32, scol, ecol, fix, bacc,
+    vt, xc, pc, pg, pgt, pgt3, hrows, hcols, hcorn, hc32, scol32, scol, ecol, fix, bacc,
     sbuf, r0, s1, r1, s2, r2, gath,
     lsem, osem, ssem, rsem, gsem,
 ):
@@ -159,7 +163,9 @@
 
     lax.fori_loop(0, rows // 4, widen_alone, 0)
     xc[0] = jnp.zeros((cols, 3 * ch), BF16)
-    xc[rows + 1] = jnp.zeros((cols, 3 * ch), BF16)
+    cells = padded_cells(rows, cols, ch)
+    for r in range(rows + 1, pl.cdiv(cells, cols)):
+        xc[r] = jnp.zeros((cols, 3 * ch), BF16)
     bacc[...] = jnp.zeros_like(bacc)
     for load in loads[1:]:
         load.wait()
@@ -285,8 +291,7 @@
     half_rows = chips * part
 
     def third(a):
-        window = xc[a : a + rows].reshape(rows * cols, 3 * ch)
-        grad = jnp.dot(pgt[...], window, preferred_element_type=F32)
+        grad = kernel_terms[a * ch : (a + 1) * ch]
         for b in range(3):
             block = grad[:, b * ch : (b + 1) * ch].T.astype(BF16)
             low = b * ch
@@ -355,11 +360,14 @@
         wg_ref[a, 1 - core] = gath[a, 1 - core].astype(F32)
         store(wg_ref.at[a], wg_hbm.at[a])
 
-    third(0)
-    third(1)
-    plane(0)
-    third(2)
-    plane(1)
+    turned = pgt[...]
+    for a in range(3):
+        ends = [jnp.zeros((ch, a * cols), BF16), jnp.zeros((ch, cells - (rows + a) * cols), BF16)]
+        pgt3[a * ch : (a + 1) * ch, :] = jnp.concatenate(([ends[0]] if a else []) + [turned, ends[1]], axis=1)
+    held = xc[...].reshape(pl.cdiv(cells, cols) * cols, 3 * ch)[:cells]
+    kernel_terms = jnp.dot(pgt3[...], held, preferred_element_type=F32)
+    for a in range(3):
+        third(a)
 
     halo_wait(1)
     widen(1, pg, pc)
@@ -371,15 +379,17 @@
         return carry
 
     steps = rows // CHUNK
-    plane(2)
+    for a in range(3):
+        plane(a)
+    lax.fori_loop(0, steps // 3, backward, 0)
     along(0)
-    lax.fori_loop(0, steps // 3, backward, 0)
     along(1)
+    along(2)
     lax.fori_loop(steps // 3, 2 * steps // 3, backward, 0)
-    along(2)
     around(0)
+    around(1)
+    around(2)
     lax.fori_loop(2 * steps // 3, steps, backward, 0)
-    around(1)
     across(0)
 
     def row_of(at_row, rhs):
@@ -392,7 +402,6 @@
     row_of(rows - 1, jnp.concatenate([vt[: 2 * third_of, :], jnp.where(bottom, near, far)], axis=0))
     store(gin_ref, gin_hbm)
 
-    around(2)
     across(1)
     finish(0)
     across(2)
@@ -423,6 +432,7 @@
     chips = (gl // 2) * gt
     n2 = (lons // gl) * (lats // gt)
     part = 3 * ch // (2 * chips)
+    cells = padded_cells(rows, cols, ch)
     limit = 62 * 1024 * 1024
     dma = pltpu.SemaphoreType.DMA
     anywhere = pl.BlockSpec(memory_space=pltpu.HBM)
@@ -446,10 +456,11 @@
             pltpu.VMEM((3, 2, chips, part, ch), F32),
             pltpu.VMEM((1, ch), F32),
             pltpu.VMEM((9 * ch, ch), BF16),
+            pltpu.VMEM((pl.cdiv(cells, cols), cols, 3 * ch), BF16),
             pltpu.VMEM((rows + 2, cols, 3 * ch), BF16),
-            pltpu.VMEM((rows + 2, cols, 3 * ch), BF16),
             pltpu.VMEM((rows, cols, ch), BF16),
             pltpu.VMEM((ch, rows * cols), BF16),
+            pltpu.VMEM((3 * ch, cells), BF16),
             pltpu.VMEM((2, 2, cols, ch), BF16),
             pltpu.VMEM((2, 2, rows, ch), BF16),
             pltpu.VMEM((2, 4, 16, ch), BF16),

time: 32.4 us -> 31.4 us (0.969)
  the two profiles are of different devices: /device:TPU:1 before, /device:TPU:0 now
where the time goes in v6:
time: 31.4 us; the launch traced here: 31.2 us
  Pallas kernels  30.6 us (97%)
  between operations  0.64 us (2%)
    pallas_call x1, Pallas kernels, shards(): pl.pallas_call(functools.partial(kernel, lons, lats), out_shape=(jax.Shap...  28.2 us
    pallas_call x1, Pallas kernels, shards(): pl.pallas_call(store_all, out_shape=(jax.ShapeDtypeStruct((rows, cols, ch...  2.34 us

profile of v6, /device:TPU:0, one launch (start us, length us, event | category | flops | bytes accessed | tf_op | source)
XLA Modules:
  0.0 31.2 jit_solution(12122699918319330557)
XLA Ops:
  0.6 28.2 %conv_silu_grads.1 = (bf16[48,48,128]{2,1,0:T(8,128)(2,1)}, bf16[48,48,128]{2,1,0:T(8,128)(2,1)}, f32[3,2,4,48,128]{4,3,2,1,0:T(8,128)}, f32[1,128]{1,0:T(1,128)}) custom-call(bf16[48,48,128]{2,1,0:T(8,128)(2,1)} %x_hbm.1, bf16[3,3,128,128]{3,2,1,0:T(8,128)(2,1)} %w_hbm.1, f32[1,128]{1,0:T(1,128)} %bitcast.3, bf16[48,48,128]{2,1,0:T(8,128)(2,1)} %c_hbm.1), custom_call_target="tpu_custom_call" | custom-call | tf_op jit(solution)/shard_map/conv_silu_grads/pallas_call | solution.py:439
  28.9 2.3 %write_results.1 = (bf16[48,48,128]{2,1,0:T(8,128)(2,1)}, bf16[48,48,128]{2,1,0:T(8,128)(2,1)}, f32[3,2,4,48,128]{4,3,2,1,0:T(8,128)}, f32[1,128]{1,0:T(1,128)}) custom-call(bf16[48,48,128]{2,1,0:T(8,128)(2,1)} %get-tuple-element.12.refs_0_, bf16[48,48,128]{2,1,0:T(8,128)(2,1)} %get-tuple-element.13.refs_1_, ...), custom_call_target="tpu_custom_call" | custom-call | tf_op jit(solution)/shard_map/write_results/pallas_call | solution.py:491

commit v7 on v6

--- a/solution.py
+++ b/solution.py
@@ -290,10 +290,9 @@
 
     half_rows = chips * part
 
-    def third(a):
-        grad = kernel_terms[a * ch : (a + 1) * ch]
+    def third(a, grad):
         for b in range(3):
-            block = grad[:, b * ch : (b + 1) * ch].T.astype(BF16)
+            block = grad[b * ch : (b + 1) * ch].T.astype(BF16)
             low = b * ch
             while low < (b + 1) * ch:
                 q = low // half_rows
@@ -353,21 +352,25 @@
     def across(a):
         wait_all(3, a, gath.at[a, core, 0 : chips - 1])
         send(4, a, gath.at[a, core], gath.at[a, core], sibling)
-        wg_ref[a, core] = gath[a, core].astype(F32)
 
     def finish(a):
         wait_all(4, a, gath.at[a, 1 - core])
-        wg_ref[a, 1 - core] = gath[a, 1 - core].astype(F32)
-        store(wg_ref.at[a], wg_hbm.at[a])
+        block = gath[a].reshape(3 * ch, ch).astype(F32)
+        for tap in range(3):
+            wg_ref[tap, a] = block[tap * ch : (tap + 1) * ch]
+        store(wg_ref.at[:, a], wg_hbm.at[:, a])
 
     turned = pgt[...]
     for a in range(3):
         ends = [jnp.zeros((ch, a * cols), BF16), jnp.zeros((ch, cells - (rows + a) * cols), BF16)]
         pgt3[a * ch : (a + 1) * ch, :] = jnp.concatenate(([ends[0]] if a else []) + [turned, ends[1]], axis=1)
     held = xc[...].reshape(pl.cdiv(cells, cols) * cols, 3 * ch)[:cells]
-    kernel_terms = jnp.dot(pgt3[...], held, preferred_element_type=F32)
-    for a in range(3):
-        third(a)
+    kernel_terms = jnp.dot(pgt3[...], held[:, : 2 * ch], preferred_element_type=F32)
+    third(0, kernel_terms[:, :ch])
+    third(1, kernel_terms[:, ch:])
+    third(2, jnp.dot(pgt3[...], held[:, 2 * ch :], preferred_element_type=F32))
+    plane(0)
+    plane(1)
 
     halo_wait(1)
     widen(1, pg, pc)
@@ -379,8 +382,7 @@
         return carry
 
     steps = rows // CHUNK
-    for a in range(3):
-        plane(a)
+    plane(2)
     lax.fori_loop(0, steps // 3, backward, 0)
     along(0)
     along(1)
@@ -441,7 +443,7 @@
         out_shape=(
             jax.ShapeDtypeStruct((rows, cols, ch), BF16),
             jax.ShapeDtypeStruct((rows, cols, ch), BF16),
-            jax.ShapeDtypeStruct((3, 2, chips, part, ch), F32),
+            jax.ShapeDtypeStruct((3, 3, ch, ch), F32),
             jax.ShapeDtypeStruct((1, ch), F32),
         ),
         in_specs=[anywhere] * 4,
@@ -453,7 +455,7 @@
             pltpu.VMEM((rows, cols, ch), BF16),
             pltpu.VMEM((rows, cols, ch), BF16),
             pltpu.VMEM((rows, cols, ch), BF16),
-            pltpu.VMEM((3, 2, chips, part, ch), F32),
+            pltpu.VMEM((3, 3, ch, ch), F32),
             pltpu.VMEM((1, ch), F32),
             pltpu.VMEM((9 * ch, ch), BF16),
             pltpu.VMEM((pl.cdiv(cells, cols), cols, 3 * ch), BF16),
@@ -493,7 +495,7 @@
         out_shape=(
             jax.ShapeDtypeStruct((rows, cols, ch), BF16),
             jax.ShapeDtypeStruct((rows, cols, ch), BF16),
-            jax.ShapeDtypeStruct((3, 2, chips, part, ch), F32),
+            jax.ShapeDtypeStruct((3, 3, ch, ch), F32),
             jax.ShapeDtypeStruct((1, ch), F32),
         ),
         in_specs=[anywhere] * 4,
@@ -501,14 +503,14 @@
         scratch_shapes=[
             pltpu.VMEM((rows, cols, ch), BF16),
             pltpu.VMEM((rows, cols, ch), BF16),
-            pltpu.VMEM((3, 2, chips, part, ch), F32),
+            pltpu.VMEM((3, 3, ch, ch), F32),
             pltpu.VMEM((1, ch), F32),
             dma((2, 4)),
         ],
         compiler_params=pltpu.CompilerParams(vmem_limit_bytes=limit),
         name="write_results",
     )(*results)
-    return outputs, input_grad, weight_grad.reshape(3, 3, ch, ch), bias_grad.reshape(ch)
+    return outputs, input_grad, weight_grad, bias_grad.reshape(ch)
 
 
 def solution(mesh):

time: 31.4 us -> 30.5 us (0.971)
  Pallas kernels: 30.6 us -> 29.7 us
    pallas_call x1, Pallas kernels: 28.2 us -> 27.4 us  [shards(): pl.pallas_call(functools.partial(kernel, lons, lats), out_shape=(jax.Shap...]
where the time goes in v7:
time: 30.5 us; the launch traced here: 30.4 us
  Pallas kernels  29.7 us (97%)
  between operations  0.64 us (2%)
    pallas_call x1, Pallas kernels, shards(): pl.pallas_call(functools.partial(kernel, lons, lats), out_shape=(jax.Shap...  27.4 us
    pallas_call x1, Pallas kernels, shards(): pl.pallas_call(store_all, out_shape=(jax.ShapeDtypeStruct((rows, cols, ch...  2.34 us

profile of v7, /device:TPU:0, one launch (start us, length us, event | category | flops | bytes accessed | tf_op | source)
XLA Modules:
  0.0 30.4 jit_solution(1957073264956218117)
XLA Ops:
  0.6 27.4 %conv_silu_grads.1 = (bf16[48,48,128]{2,1,0:T(8,128)(2,1)}, bf16[48,48,128]{2,1,0:T(8,128)(2,1)}, f32[3,3,128,128]{3,2,1,0:T(8,128)}, f32[1,128]{1,0:T(1,128)}) custom-call(bf16[48,48,128]{2,1,0:T(8,128)(2,1)} %x_hbm.1, bf16[3,3,128,128]{3,2,1,0:T(8,128)(2,1)} %w_hbm.1, f32[1,128]{1,0:T(1,128)} %bitcast.2, bf16[48,48,128]{2,1,0:T(8,128)(2,1)} %c_hbm.1), custom_call_target="tpu_custom_call" | custom-call | tf_op jit(solution)/shard_map/conv_silu_grads/pallas_call | solution.py:441
  28.0 2.3 %write_results.1 = (bf16[48,48,128]{2,1,0:T(8,128)(2,1)}, bf16[48,48,128]{2,1,0:T(8,128)(2,1)}, f32[3,3,128,128]{3,2,1,0:T(8,128)}, f32[1,128]{1,0:T(1,128)}) custom-call(bf16[48,48,128]{2,1,0:T(8,128)(2,1)} %get-tuple-element.12.refs_0_, bf16[48,48,128]{2,1,0:T(8,128)(2,1)} %get-tuple-element.13.refs_1_, f32[3,3,128,128]{3,2,1,0:T(8,128)} %get-tuple-element.14.refs_2_, ...), custom_call_target="tpu_custom_call" | custom-call | tf_op jit(solution)/shard_map/write_results/pallas_call | solution.py:493
